TPU v7x, 32 devices: a whole 2x2x4 slice. The times are simulated.
32 devices in a mesh: chan: 8 (over z, x), mode: 4 (over y, core).
Axes of the slice: x: 2, y: 2, z: 4, core: 2. Of those that a mesh axis runs over, the one named last changes fastest.
Arguments:
- weight: bfloat16 [512, 2, 32, 32, 256], P('chan', None, 'mode'), may hold values from -0.59765625 to 0.59765625
- gradient: bfloat16 [512, 2, 32, 32, 256], P('chan', None, 'mode'), may hold values from -6 to 6
- first_moment: float32 [128, 2, 16, 16, 128], P('chan', None, None, 'mode'), may hold values from -2 to 2
- second_moment: float32 [128, 2, 16, 16, 128], P('chan', None, None, 'mode'), may hold values from 0.0005 to 0.02
- u_in: float32 [512, 128], P('chan'), may hold values from -0.25 to 0.25
- u_out: bfloat16 [256, 128], replicated, may hold values from -0.375 to 0.375
- u_modes_a: float32 [32, 16], replicated, may hold values from -1 to 1
- u_modes_b: float32 [32, 16], replicated, may hold values from -1 to 1
Outputs:
- new_weight: bfloat16 [512, 2, 32, 32, 256], P('chan', None, 'mode')
- new_first: float32 [128, 2, 16, 16, 128], P('chan', None, None, 'mode')
- new_second: float32 [128, 2, 16, 16, 128], P('chan', None, None, 'mode')
All inputs are finite; a program needn't handle non-finite values.
Results may differ from a plain program's by a relative error of at most 0.004.
Values sent between devices are 32-bit elements; how exact they have to be, the bound alone decides.
A program may use at most 128 MiB of HBM per device.

v0:
```python
import jax
import jax.numpy as jnp
from jax import lax
from jax.sharding import PartitionSpec as P

STEP = 4


HIGH = lax.Precision.HIGHEST
beta_one = 0.9
beta_two = 0.999
step_rate = 0.5


def shards(weight, gradient, first_moment, second_moment, u_in, u_out, u_modes_a, u_modes_b):
    local_in, parts, local_a, modes_b, out_ch = gradient.shape
    rank_out = u_out.shape[1]
    reduced = jnp.dot(gradient.reshape(-1, out_ch), u_out, preferred_element_type=jnp.float32)
    reduced = reduced.reshape(local_in, parts, local_a, modes_b, rank_out)
    narrowed = jnp.einsum("ipabo,bs->ipaso", reduced, u_modes_b, precision=HIGH)
    local_rows = lax.dynamic_slice_in_dim(u_modes_a, lax.axis_index("mode") * local_a, local_a, 0)
    columns = u_in
    share = lax.psum_scatter(
        jnp.einsum("ik,ipaso->kpaso", columns, narrowed, precision=HIGH),
        "chan",
        scatter_dimension=0,
        tiled=True,
    )
    arranged = lax.all_to_all(share, "mode", split_axis=3, concat_axis=2, tiled=True)
    core = jnp.einsum("kpaso,ar->kprso", arranged, u_modes_a, precision=HIGH)
    new_first = beta_one * first_moment + (1.0 - beta_one) * core
    new_second = beta_two * second_moment + (1.0 - beta_two) * core * core
    direction = (
        new_first / (1.0 - beta_one**STEP) / (jnp.sqrt(new_second / (1.0 - beta_two**STEP)) + 1e-08)
    )
    columns = u_in
    spread = jnp.einsum(
        "ik,kprso->iprso",
        columns,
        lax.all_gather(direction, "chan", axis=0, tiled=True),
        precision=HIGH,
    )
    full_ranks = lax.all_gather(spread, "mode", axis=3, tiled=True)
    wide = jnp.einsum("iprso,ar->ipaso", full_ranks, local_rows, precision=HIGH)
    expanded = jnp.einsum("ipaso,bs->ipabo", wide, u_modes_b, precision=HIGH).astype(jnp.bfloat16)
    update = jnp.dot(expanded.reshape(-1, rank_out), u_out.T, preferred_element_type=jnp.float32)
    update = update.reshape(weight.shape)
    new_weight = (weight.astype(jnp.float32) - step_rate * update).astype(jnp.bfloat16)
    return (new_weight, new_first, new_second)


def solution(mesh):
    in_specs = (
        P("chan", None, "mode", None, None),
        P("chan", None, "mode", None, None),
        P("chan", None, None, "mode", None),
        P("chan", None, None, "mode", None),
        P("chan", None),
        P(),
        P(),
        P(),
    )
    out_specs = (
        P("chan", None, "mode", None, None),
        P("chan", None, None, "mode", None),
        P("chan", None, None, "mode", None),
    )
    return jax.shard_map(shards, mesh=mesh, in_specs=in_specs, out_specs=out_specs, check_vma=False)
```

profile of v0, /device:TPU:0, one launch (start us, length us, event | category | flops | bytes accessed | tf_op | source)
XLA Modules:
  0.0 687.3 jit_solution(12558415093577222684)
XLA Ops:
  7.2 0.0 copy-start
  7.2 0.0 copy-start.4
  7.2 0.0 reduce-scatter.2.cloned.1.call-start
  7.2 0.8 copy-done
  8.0 9.3 %fusion.28 = f32[64,2,8,32,128]{4,3,2,1,0:T(8,128)S(1)} fusion(bf16[64,2,8,32,256]{4,3,2,1,0:T(8,128)(2,1)} %param.9, bf16[256,128]{1,0:T(8,128)(2,1)S(1)} %copy-done), kind=kOutput, calls=%fused_computation.26 | convolution fusion | flops 2147483648 | bytes 33619968 | tf_op jit(solution)/shard_map/dot_general | solution.py:18
  17.3 0.0 copy-done.4
  17.3 0.0 copy-start.2
  17.4 10.4 %convolution_bitcast_fusion = f32[64,2,8,16,128]{4,3,2,1,0:T(8,128)S(1)} fusion(f32[64,2,8,32,128]{4,3,2,1,0:T(8,128)S(1)} %fusion.28, f32[32,16]{0,1:T(8,128)S(1)} %copy-done.4), kind=kOutput, calls=%fused_computation.13 | convolution fusion | flops 805306368 | bytes 25167872 | tf_op jit(solution)/shard_map/ipabo,bs->ipaso/dot_general | solution.py:20
  27.8 0.0 copy-done.2
  27.8 30.3 %fusion.10 = f32[128,2,8,16,128]{0,4,3,2,1:T(8,128)} fusion(f32[64,2,8,16,128]{4,3,2,1,0:T(8,128)S(1)} %convolution_bitcast_fusion, f32[64,128]{1,0:T(8,128)S(1)} %copy-done.2), kind=kOutput, calls=%fused_computation.11 | convolution fusion | flops 3221225472 | bytes 25198592 | tf_op jit(solution)/shard_map/ik,ipaso->kpaso/dot_general | solution.py:24
  58.0 17.4 %copy.52 = f32[128,2,8,16,128]{4,3,2,1,0:T(8,128)} copy(f32[128,2,8,16,128]{0,4,3,2,1:T(8,128)} %fusion.10) | data formatting | bytes 33554432 | tf_op jit(solution)/shard_map/ik,ipaso->kpaso/dot_general | solution.py:24
  75.4 0.0 reduce-scatter.2.cloned.1.call-update
  75.4 0.0 copy-start.1
  75.5 0.0 copy-start.3
  75.5 0.0 all-gather.3.cloned.1.call-start
  75.5 285.4 %reduce-scatter.2.cloned.1.call-done = f32[16,2,8,16,128]{4,3,2,1,0:T(8,128)} async-done(((f32[128,2,8,16,128]{4,3,2,1,0:T(8,128)}), f32[16,2,8,16,128]{4,3,2,1,0:T(8,128)}) %reduce-scatter.2.cloned.1.call-update) | async-done | bytes 2097168 | tf_op jit(solution)/shard_map/reduce_scatter | solution.py:23
  361.0 2.3 copy.53
  363.2 28.2 %all_to_all.18 = f32[16,2,8,16,128]{4,2,1,0,3:T(8,128)S(1)} all-to-all(f32[16,2,8,16,128]{4,2,1,0,3:T(8,128)S(1)} %copy.53), channel_id=1, replica_groups=mesh['chan'=8,'mode'=4] {'mode'}, dimensions={3} | all-to-all | bytes 4194304 | tf_op jit(solution)/shard_map/all_to_all | solution.py:29
  391.4 0.0 copy-done.1
  391.4 0.0 copy-done.3
  391.4 4.0 add_divide_fusion
  395.5 0.0 all-gather.3.cloned.1.call-update
  395.5 0.0 all-gather.5.cloned.1.call-start
  395.5 123.2 %all-gather.3.cloned.1.call-done = f32[128,2,16,4,128]{4,2,3,1,0:T(8,128)} async-done(((f32[16,2,16,4,128]{4,2,3,1,0:T(8,128)}), f32[128,2,16,4,128]{4,2,3,1,0:T(8,128)}) %all-gather.3.cloned.1.call-update) | async-done | bytes 8388624 | tf_op jit(solution)/shard_map/all_gather | solution.py:40
  518.7 12.7 %fusion.16 = f32[64,2,16,4,128]{4,0,3,2,1:T(8,128)S(1)} fusion(f32[128,2,16,4,128]{4,2,3,1,0:T(8,128)} %all-gather.3.cloned.1.call-done, f32[64,128]{1,0:T(8,128)S(1)} %copy-done.2), kind=kOutput, calls=%fused_computation.14 | convolution fusion | flops 1610612736 | bytes 12615680 | tf_op jit(solution)/shard_map/ik,kprso->iprso/dot_general | solution.py:37
  531.4 4.4 copy.57
  535.8 0.0 all-gather.5.cloned.1.call-update
  535.8 1.4 copy.60
  537.2 1.4 copy.61
  538.6 101.5 %all-gather.5.cloned.1.call-done = f32[64,2,16,16,128]{4,2,1,0,3:T(8,128)} async-done(((f32[64,2,16,4,128]{4,2,1,0,3:T(8,128)}), f32[64,2,16,16,128]{4,2,1,0,3:T(8,128)}) %all-gather.5.cloned.1.call-update) | async-done | bytes 16777232 | tf_op jit(solution)/shard_map/all_gather | solution.py:43
  640.1 10.9 %fusion.13 = f32[64,2,8,16,128]{4,2,3,1,0:T(8,128)S(1)} fusion(f32[64,2,16,16,128]{4,2,1,0,3:T(8,128)} %all-gather.5.cloned.1.call-done, f32[32,16]{0,1:T(8,128)S(1)} %copy-done.3, s32[]{:T(128)S(6)} %select_n.3), kind=kOutput, calls=%fused_computation.12 | convolution fusion | flops 402653184 | bytes 25167876 | tf_op jit(solution)/shard_map/iprso,ar->ipaso/dot_general | solution.py:44
  651.0 15.6 %fusion.3 = bf16[64,2,8,128,32]{3,4,2,1,0:T(8,128)(2,1)} fusion(f32[64,2,8,16,128]{4,2,3,1,0:T(8,128)S(1)} %fusion.13, f32[32,16]{0,1:T(8,128)S(1)} %copy-done.4), kind=kOutput, calls=%fused_computation.4 | convolution fusion | flops 805306368 | bytes 16779264 | tf_op jit(solution)/shard_map/ipaso,bs->ipabo/dot_general | solution.py:45
  666.7 14.1 %subtract_convert_fusion = bf16[64,2,8,32,256]{4,3,2,1,0:T(8,128)(2,1)} fusion(bf16[64,2,8,32,256]{4,3,2,1,0:T(8,128)(2,1)} %param.8, bf16[64,2,8,128,32]{3,4,2,1,0:T(8,128)(2,1)} %fusion.3, bf16[256,128]{1,0:T(8,128)(2,1)S(1)} %copy-done), kind=kOutput, calls=%fused_computation | convolution fusion | flops 2181038080 | bytes 42008576 | tf_op jit(solution)/shard_map/dot_general | solution.py:46
Async XLA Ops:
  7.2 0.8 copy-start
  7.2 10.2 %copy-start.4 = (f32[32,16]{0,1:T(8,128)S(1)}, f32[32,16]{0,1:T(8,128)}, u32[]{:S(2)}) copy-start(f32[32,16]{0,1:T(8,128)} %param.15) | copy-start | bytes 6148
  7.2 353.8 %reduce-scatter.2.cloned.1.call-start = ((), (), s32[]{:S(2)}) async-start(), calls=%async_computation.2 | async-start | bytes 18874368 | tf_op jit(solution)/shard_map/reduce_scatter | solution.py:23
  17.3 10.4 %copy-start.2 = (f32[64,128]{1,0:T(8,128)S(1)}, f32[64,128]{1,0:T(8,128)}, u32[]{:S(2)}) copy-start(f32[64,128]{1,0:T(8,128)} %param.12) | copy-start | bytes 98308
  75.4 316.0 %copy-start.1 = (f32[16,2,16,4,128]{4,3,2,1,0:T(4,128)S(1)}, f32[16,2,16,4,128]{4,3,2,1,0:T(4,128)}, u32[]{:S(2)}) copy-start(f32[16,2,16,4,128]{4,3,2,1,0:T(4,128)} %param.10) | copy-start | bytes 3145732
  75.5 316.0 %copy-start.3 = (f32[32,16]{0,1:T(8,128)S(1)}, f32[32,16]{0,1:T(8,128)}, u32[]{:S(2)}) copy-start(f32[32,16]{0,1:T(8,128)} %param.14) | copy-start | bytes 6148
  75.5 443.2 %all-gather.3.cloned.1.call-start = ((), (), s32[]{:S(2)}) async-start(), calls=%async_computation.3 | async-start | bytes 9437184 | tf_op jit(solution)/shard_map/all_gather | solution.py:40
  395.5 244.6 %all-gather.5.cloned.1.call-start = ((), (), s32[]{:S(2)}) async-start(), calls=%async_computation.4 | async-start | bytes 20971520 | tf_op jit(solution)/shard_map/all_gather | solution.py:43
Sparse Core Ops, SparseCore 0:
  75.6 285.3 reduce-scatter.1
  395.6 123.0 all-gather.2
  536.0 104.0 all-gather.4
where the time goes:
time: 688 us; the launch traced here: 687 us
  waiting for transfers between devices  510 us (74%)
  matrix products  107 us (16%)
  blocking collectives  28.2 us (4%)
  local copies, waits for them, and re-layouts  27.7 us (4%)
  between operations  13.8 us (2%)
    reduce_scatter x1, waiting for transfers between devices, shards(): lax.psum_scatter(jnp.einsum('ik,ipaso->kpaso', columns, narrowed, precisi...  285 us
    all_gather x1, waiting for transfers between devices, shards(): lax.all_gather(direction, 'chan', axis=0, tiled=True)  123 us
    all_gather x1, waiting for transfers between devices, shards(): full_ranks = lax.all_gather(spread, 'mode', axis=3, tiled=True)  101 us
    dot_general x1, matrix products, shards(): jnp.einsum('ik,ipaso->kpaso', columns, narrowed, precision=HIGH)  30.3 us
    all_to_all x1, blocking collectives, shards(): lax.all_to_all(share, 'mode', split_axis=3, concat_axis=2, tiled=True)  28.2 us
    dot_general x1, local copies, waits for them, and re-layouts, shards(): jnp.einsum('ik,ipaso->kpaso', columns, narrowed, precision=HIGH)  17.4 us
    dot_general x1, matrix products, shards(): jnp.einsum('ipaso,bs->ipabo', wide, u_modes_b, precision=HIGH)  15.6 us
    dot_general x1, matrix products, shards(): jnp.dot(expanded.reshape(-1, rank_out), u_out.T, preferred_element_type=j...  14.1 us
  transfers between devices with their start and end apart: 3, of which 3 were waited for; matrix products, arithmetic and copies ran while one was open for 0% of the time, Pallas kernels for 0%

commit v1 on v0

v1 whole, which is shorter than its diff:
```python
import functools

import jax
import jax.numpy as jnp
from jax import lax
from jax.experimental import pallas as pl
from jax.experimental.pallas import tpu as pltpu
from jax.sharding import PartitionSpec as P

STEP = 4
BETA_ONE = 0.9
BETA_TWO = 0.999
STEP_RATE = 0.5
F32 = jnp.float32
BF16 = jnp.bfloat16
ROWS = 8
GROUPS = 2


def split(value):
    high = value.astype(BF16)
    return high, (value - high.astype(F32)).astype(BF16)


def dot(left, right):
    return jnp.dot(left, right, preferred_element_type=F32)


def dot3(left, right):
    left_high, left_low = left
    right_high, right_low = split(right)
    return dot(left_high, right_high) + (dot(left_high, right_low) + dot(left_low, right_high))


def turn(value, start):
    twice = jnp.concatenate([value, value])
    return lax.dynamic_slice_in_dim(twice, start, value.shape[0], 0)


def turn_back(value, start):
    return turn(value[::-1], value.shape[0] - 1 - start)


def call(body, grid, in_specs, out_specs, out_shape, scratch, flops, size):
    return pl.pallas_call(
        body,
        grid=grid,
        in_specs=in_specs,
        out_specs=out_specs,
        out_shape=out_shape,
        scratch_shapes=scratch,
        compiler_params=pltpu.CompilerParams(vmem_limit_bytes=40 * 1024 * 1024),
        cost_estimate=pl.CostEstimate(flops=flops, bytes_accessed=size, transcendentals=0),
    )


def narrow(gradient, u_out, select, part, modes, groups):
    ins, _, local_a, modes_b, out_ch = gradient.shape
    rank_out = u_out.shape[1]
    ranks = select.shape[0] // (ROWS * modes)
    each = ranks // groups

    def body(grad_ref, factor_ref, select_ref, *outs):
        matrix = split(select_ref[...])
        factor = factor_ref[...]
        for block in range(ins // ROWS):
            rows = pl.ds(block * ROWS, ROWS)
            lines = grad_ref[rows, 0, 0].reshape(ROWS * modes_b, out_ch)
            done = dot3(matrix, dot(lines, factor)).reshape(modes, groups, each, ROWS, rank_out)
            for peer in range(modes):
                for group in range(groups):
                    outs[peer * groups + group][0, :, rows, :] = done[peer, group]

    count = modes * groups
    spec = pl.BlockSpec((1, each, ins, rank_out), lambda a: (a, 0, 0, 0))
    shape = jax.ShapeDtypeStruct((local_a, each, ins, rank_out), F32)
    return call(
        body,
        (local_a,),
        [
            pl.BlockSpec((ins, 1, 1, modes_b, out_ch), lambda a: (0, part, a, 0, 0)),
            pl.BlockSpec(u_out.shape, lambda a: (0, 0)),
            pl.BlockSpec(select.shape, lambda a: (0, 0)),
        ],
        [spec] * count,
        [shape] * count,
        [],
        2 * ins * local_a * modes_b * out_ch * rank_out * 4,
        ins * local_a * modes_b * out_ch * 3,
    )(gradient, u_out, select)


def gather_core(pieces, select, columns, rank_a, across, along):
    modes = len(pieces)
    local_a, each, ins, rank_out = pieces[0].shape
    rank_in = columns.shape[0]
    own = rank_in // (across * along)

    def body(*refs):
        xs, select_ref, columns_ref = refs[:modes], refs[modes], refs[modes + 1]
        outs, mixed = refs[modes + 2 : -1], refs[-1]
        matrix = split(select_ref[...])
        for block in range(ins // ROWS):
            rows = pl.ds(block * ROWS, ROWS)
            lines = jnp.concatenate(
                [x[:, 0, rows, :].reshape(local_a * ROWS, rank_out) for x in xs], axis=0
            )
            done = dot3(matrix, lines)
            for r in range(rank_a):
                mixed[rows, r * rank_out : (r + 1) * rank_out] = done[r * ROWS : (r + 1) * ROWS]
        left = split(columns_ref[...])
        for r in range(rank_a):
            done = dot3(left, mixed[:, r * rank_out : (r + 1) * rank_out])
            done = done.reshape(across, along, own, rank_out)
            for x in range(across):
                outs[x][:, r, 0] = done[x]

    return call(
        body,
        (each,),
        [pl.BlockSpec((local_a, 1, ins, rank_out), lambda s: (0, s, 0, 0))] * modes
        + [pl.BlockSpec(select.shape, lambda s: (0, 0)), pl.BlockSpec(columns.shape, lambda s: (0, 0))],
        [pl.BlockSpec((along, rank_a, 1, own, rank_out), lambda s: (0, 0, s, 0, 0))] * across,
        [jax.ShapeDtypeStruct((along, rank_a, each, own, rank_out), F32)] * across,
        [pltpu.VMEM((ins, rank_a * rank_out), F32)],
        2 * each * rank_a * ins * rank_in * rank_out * 6,
        4 * each * rank_out * (modes * local_a * ins + rank_in * rank_a),
    )(*pieces, select, columns)


def spread_back(pieces, select, columns, modes):
    across = len(pieces)
    along, rank_a, each, own, rank_out = pieces[0].shape
    ins = columns.shape[0]
    local_a = select.shape[0] // (ROWS * modes)

    def body(*refs):
        xs, select_ref, columns_ref = refs[:across], refs[across], refs[across + 1]
        outs, spread = refs[across + 2 : -1], refs[-1]
        left = split(columns_ref[...])
        for r in range(rank_a):
            lines = jnp.concatenate(
                [x[:, r, 0].reshape(along * own, rank_out) for x in xs], axis=0
            )
            spread[r] = dot3(left, lines)
        matrix = split(select_ref[...])
        for block in range(ins // ROWS):
            rows = pl.ds(block * ROWS, ROWS)
            done = dot3(matrix, spread[:, rows, :].reshape(rank_a * ROWS, rank_out))
            done = done.reshape(modes, local_a, ROWS, rank_out)
            for peer in range(modes):
                outs[peer][:, 0, rows, :] = done[peer]

    return call(
        body,
        (each,),
        [pl.BlockSpec((along, rank_a, 1, own, rank_out), lambda s: (0, 0, s, 0, 0))] * across
        + [pl.BlockSpec(select.shape, lambda s: (0, 0)), pl.BlockSpec(columns.shape, lambda s: (0, 0))],
        [pl.BlockSpec((local_a, 1, ins, rank_out), lambda s: (0, s, 0, 0))] * modes,
        [jax.ShapeDtypeStruct((local_a, each, ins, rank_out), F32)] * modes,
        [pltpu.VMEM((rank_a, ins, rank_out), F32)],
        2 * each * rank_a * ins * columns.shape[1] * rank_out * 6,
        4 * each * rank_out * (modes * local_a * ins + columns.shape[1] * rank_a),
    )(*pieces, select, columns)


def update(weight, pieces, back, select, previous, part, groups):
    ins, _, local_a, modes_b, out_ch = weight.shape
    count = len(pieces)
    each, rank_out = pieces[0].shape[1], pieces[0].shape[3]
    extra = [] if previous is None else [previous]

    def body(weight_ref, *refs):
        xs, back_ref, select_ref, out_ref = refs[:count], refs[count], refs[count + 1], refs[-1]
        matrix = split(select_ref[...])
        factor = back_ref[...]
        for block in range(ins // ROWS):
            rows = pl.ds(block * ROWS, ROWS)
            lines = jnp.concatenate(
                [x[0, :, rows, :].reshape(each * ROWS, rank_out) for x in xs], axis=0
            )
            expanded = dot3(matrix, lines).astype(BF16)
            change = dot(expanded, factor).reshape(ROWS, modes_b, out_ch)
            old = weight_ref[rows, 0, 0].astype(F32)
            out_ref[rows, 0, 0] = (old - STEP_RATE * change).astype(BF16)

    spec = pl.BlockSpec((ins, 1, 1, modes_b, out_ch), lambda a: (0, part, a, 0, 0))
    return pl.pallas_call(
        body,
        grid=(local_a,),
        in_specs=[spec]
        + [pl.BlockSpec((1, each, ins, rank_out), lambda a: (a, 0, 0, 0))] * count
        + [pl.BlockSpec(back.shape, lambda a: (0, 0)), pl.BlockSpec(select.shape, lambda a: (0, 0))]
        + [pl.BlockSpec(memory_space=pl.ANY)] * len(extra),
        out_specs=spec,
        out_shape=jax.ShapeDtypeStruct(weight.shape, BF16),
        input_output_aliases={} if previous is None else {count + 3: 0},
        compiler_params=pltpu.CompilerParams(vmem_limit_bytes=40 * 1024 * 1024),
        cost_estimate=pl.CostEstimate(
            flops=2 * ins * local_a * modes_b * out_ch * rank_out * 4,
            bytes_accessed=ins * local_a * modes_b * out_ch * 5,
            transcendentals=0,
        ),
    )(weight, *pieces, back, select, *extra)


def shards(chan, modes, weight, gradient, first_moment, second_moment, u_in, u_out, u_modes_a, u_modes_b):
    ins, parts, local_a, modes_b, out_ch = gradient.shape
    own, _, rank_a, ranks, rank_out = first_moment.shape
    groups = GROUPS if ranks % GROUPS == 0 else 1
    across = max(d for d in range(1, chan + 1) if chan % d == 0 and d * d <= chan)
    along = chan // across
    here = lax.axis_index("chan")
    mode = lax.axis_index("mode")
    z, x = here // across, here % across
    eye = jnp.eye(ROWS, dtype=F32)

    factor_b = u_modes_b.T.reshape(modes, groups, ranks // groups, modes_b)
    factor_a = u_modes_a.reshape(modes, local_a, rank_a)
    narrow_b = jnp.einsum("dgsb,ij->dgsijb", turn(factor_b, mode), eye, precision="highest")
    narrow_b = narrow_b.reshape(modes * ranks * ROWS, ROWS * modes_b)
    widen_b = jnp.einsum("dgsb,ij->jbdgsi", turn_back(factor_b, mode), eye, precision="highest")
    widen_b = widen_b.reshape(ROWS * modes_b, modes * ranks * ROWS)
    narrow_a = jnp.einsum("dar,ij->ridaj", turn_back(factor_a, mode), eye, precision="highest")
    narrow_a = narrow_a.reshape(rank_a * ROWS, modes * local_a * ROWS)
    widen_a = jnp.einsum("dar,ij->dairj", turn(factor_a, mode), eye, precision="highest")
    widen_a = widen_a.reshape(modes * local_a * ROWS, rank_a * ROWS)

    columns = u_in.reshape(ins, along, across, own).transpose(2, 1, 3, 0)
    forward_columns = turn(columns, x).reshape(-1, ins)
    turned = turn(turn_back(columns, x).transpose(1, 0, 2, 3), z).transpose(1, 0, 2, 3)
    backward_columns = turned.reshape(-1, ins).T

    def to_mode(value, d):
        if d == 0:
            return value
        return lax.ppermute(value, "mode", [(m, (m + d) % modes) for m in range(modes)])

    def to_across(value, d):
        pairs = [
            (q * across + c, q * across + (c + d) % across)
            for q in range(along)
            for c in range(across)
        ]
        return lax.ppermute(value, "chan", pairs)

    def to_along(value, sign, sources):
        pairs = [
            (q * across + c, (q + sign) * across + c) for q in sources for c in range(across)
        ]
        return lax.ppermute(value, "chan", pairs)

    def scatter(held):
        arrived = [held[0]] + [to_across(held[d], d) for d in range(1, across)]

        def local(q):
            q = jnp.clip(q, 0, along - 1)
            terms = [lax.dynamic_index_in_dim(v, q, 0, keepdims=False) for v in arrived]
            return functools.reduce(jnp.add, terms)

        right = left = None
        last = along - 1
        for t in range(last):
            send_right, send_left = local(last - t + z), local(t - last + z)
            if t > 0:
                send_right, send_left = send_right + right, send_left + left
            right = to_along(send_right, 1, range(t + 1))
            left = to_along(send_left, -1, range(last - t, along))
        total = local(z)
        return total if last == 0 else total + right + left

    def gather(value):
        last = along - 1
        rights, lefts = [], []
        right = left = value
        for t in range(last):
            right = to_along(right, 1, range(t, last))
            left = to_along(left, -1, range(1, along - t))
            rights.append(right)
            lefts.append(left)
        slots = [value] + [lefts[j - 1] + rights[last - j] for j in range(1, along)]
        full = jnp.stack(slots)
        return [full] + [to_across(full, d) for d in range(1, across)]

    shares = {}
    for p in range(parts):
        narrowed = narrow(gradient, u_out, narrow_b, p, modes, groups)
        for g in range(groups):
            pieces = [to_mode(narrowed[d * groups + g], d) for d in range(modes)]
            held = gather_core(pieces, narrow_a, forward_columns, rank_a, across, along)
            shares[p, g] = scatter(held)

    wides, firsts, seconds = {}, [], []
    each = ranks // groups
    for p in range(parts):
        first_parts, second_parts = [], []
        for g in range(groups):
            core = shares[p, g].transpose(2, 0, 1, 3)
            old_first = first_moment[:, p, :, g * each : (g + 1) * each]
            old_second = second_moment[:, p, :, g * each : (g + 1) * each]
            new_first = BETA_ONE * old_first + (1.0 - BETA_ONE) * core
            new_second = BETA_TWO * old_second + (1.0 - BETA_TWO) * core * core
            direction = (
                new_first
                / (1.0 - BETA_ONE**STEP)
                / (jnp.sqrt(new_second / (1.0 - BETA_TWO**STEP)) + 1e-08)
            )
            first_parts.append(new_first)
            second_parts.append(new_second)
            pieces = gather(direction.transpose(1, 2, 0, 3))
            outs = spread_back(pieces, widen_a, backward_columns, modes)
            for d in range(modes):
                wides[p, d, g] = to_mode(outs[d], d)
        firsts.append(jnp.concatenate(first_parts, axis=2))
        seconds.append(jnp.concatenate(second_parts, axis=2))

    new_weight = None
    back = u_out.T
    for p in range(parts):
        pieces = [wides[p, d, g] for d in range(modes) for g in range(groups)]
        new_weight = update(weight, pieces, back, widen_b, new_weight, p, groups)
    return (new_weight, jnp.stack(firsts, axis=1), jnp.stack(seconds, axis=1))


def solution(mesh):
    wide = P("chan", None, "mode", None, None)
    core = P("chan", None, None, "mode", None)
    body = functools.partial(shards, mesh.shape["chan"], mesh.shape["mode"])
    return jax.shard_map(
        body,
        mesh=mesh,
        in_specs=(wide, wide, core, core, P("chan", None), P(), P(), P()),
        out_specs=(wide, core, core),
        check_vma=False,
    )
```

time: 688 us -> 525 us (0.76)
  waiting for transfers between devices: 510 us -> 188 us
  starting transfers between devices: 0.12 us -> 167 us
  Pallas kernels: 0 us -> 111 us
  matrix products: 107 us -> 0 us
  other arithmetic: 0 us -> 30.7 us
  blocking collectives: 28.2 us -> 0 us
  between operations: 13.8 us -> 2.05 us
    reduce_scatter x1 -> x0, waiting for transfers between devices: 285 us -> none  [shards(): lax.psum_scatter(jnp.einsum('ik,ipaso->kpaso', columns, narrowed, precisi...]
    all_gather x2 -> x0, waiting for transfers between devices: 225 us -> none  [the longest x1 123 us: shards(): lax.all_gather(direction, 'chan', axis=0, tiled=True)]
    ppermute x0 -> x80, waiting for transfers between devices: none -> 188 us  [the longest x8 104 us: to_across(): return lax.ppermute(value, 'chan', pairs)]
    ppermute x0 -> x80, starting transfers between devices: none -> 167 us  [the longest x48 125 us: to_along(): return lax.ppermute(value, 'chan', pairs)]
    pallas_call x0 -> x12, Pallas kernels: none -> 111 us  [the longest x2 40.4 us: narrow(): call(body, (local_a,), [pl.BlockSpec((ins, 1, 1, modes_b, out_ch), lambda...]
    dot_general x8 -> x0, matrix products: 107 us -> none  [the longest x1 30.3 us: shards(): jnp.einsum('ik,ipaso->kpaso', columns, narrowed, precision=HIGH)]
    all_to_all x1 -> x0, blocking collectives: 28.2 us -> none  [shards(): lax.all_to_all(share, 'mode', split_axis=3, concat_axis=2, tiled=True)]
    dot_general x2 -> x0, local copies, waits for them, and re-layouts: 21.8 us -> none  [the longest x1 17.4 us: shards(): jnp.einsum('ik,ipaso->kpaso', columns, narrowed, precision=HIGH)]
  transfers between devices with their start and end apart: 3 -> 80, of which waited for: 3 -> 22; matrix products, arithmetic and copies ran while one was open for 0% -> 9% of each run, Pallas kernels for 0% -> 14%
where the time goes in v1:
time: 525 us; the launch traced here: 521 us
  waiting for transfers between devices  188 us (36%)
  starting transfers between devices  167 us (32%)
  Pallas kernels  111 us (21%)
  other arithmetic  30.7 us (6%)
  local copies, waits for them, and re-layouts  23.5 us (4%)
    ppermute x48, starting transfers between devices, to_along(): return lax.ppermute(value, 'chan', pairs)  125 us
    ppermute x8, waiting for transfers between devices, to_across(): return lax.ppermute(value, 'chan', pairs)  104 us
    ppermute x24, waiting for transfers between devices, to_mode(): lax.ppermute(value, 'mode', [(m, (m + d) % modes) for m in range(modes)])  57.7 us
    pallas_call x2, Pallas kernels, narrow(): call(body, (local_a,), [pl.BlockSpec((ins, 1, 1, modes_b, out_ch), lambda...  40.4 us
    pallas_call x2, Pallas kernels, update(): pl.pallas_call(body, grid=(local_a,), in_specs=[spec] + [pl.BlockSpec((1,...  39.8 us
    ppermute x24, starting transfers between devices, to_mode(): lax.ppermute(value, 'mode', [(m, (m + d) % modes) for m in range(modes)])  29.6 us
    ppermute x48, waiting for transfers between devices, to_along(): return lax.ppermute(value, 'chan', pairs)  25.8 us
    pallas_call x4, Pallas kernels, gather_core(): call(body, (each,), [pl.BlockSpec((local_a, 1, ins, rank_out), lambda s:...  15.9 us
  transfers between devices with their start and end apart: 80, of which 22 were waited for; matrix products, arithmetic and copies ran while one was open for 9% of the time, Pallas kernels for 14%

profile of v1, /device:TPU:0, one launch (start us, length us, event | category | flops | bytes accessed | tf_op | source)
XLA Modules:
  0.0 521.4 jit_solution(8892817670263027348)
XLA Ops:
  4.1 20.3 %shard_map.108 = (f32[8,2,64,128]{3,2,1,0:T(8,128)S(1)}, f32[8,2,64,128]{3,2,1,0:T(8,128)S(1)}, f32[8,2,64,128]{3,2,1,0:T(8,128)S(1)}, f32[8,2,64,128]{3,2,1,0:T...) custom-call(bf16[64,2,8,32,256]{4,3,2,1,0:T(8,128)(2,1)} %grad_ref.3, ...), custom_call_target="tpu_custom_call" | custom-call | flops 4294967296 | bytes 12582912 | tf_op jit(solution)/shard_map/pallas_call | solution.py:77
  24.8 2.6 collective-permute-start.41
  28.8 4.7 collective-permute-start.57
  33.5 5.7 %collective-permute-start.58 = (f32[8,2,64,128]{3,2,1,0:T(8,128)}, f32[8,2,64,128]{3,2,1,0:T(8,128)}, u32[]{:S(2)}, u32[]{:S(2)}) collective-permute-start(f32[8,2,64,128]{3,2,1,0:T(8,128)} %get-tuple-element.72), channel_id=1, source_target_pairs={{0,2},{1,3},{2,0},{3,1},{4,6},{5,7},{6,4},{7,5},{8,10},{9,11},{10,... | collective-permute-start | bytes 1572872 | tf_op jit(solution)/shard_map/ppermute | solution.py:237
  39.2 20.2 %shard_map.103 = (f32[8,2,64,128]{3,2,1,0:T(8,128)S(1)}, f32[8,2,64,128]{3,2,1,0:T(8,128)S(1)}, f32[8,2,64,128]{3,2,1,0:T(8,128)S(1)}, f32[8,2,64,128]{3,2,1,0:T...) custom-call(bf16[64,2,8,32,256]{4,3,2,1,0:T(8,128)(2,1)} %grad_ref.3, ...), custom_call_target="tpu_custom_call" | custom-call | flops 4294967296 | bytes 12582912 | tf_op jit(solution)/shard_map/pallas_call | solution.py:77
  61.8 1.7 collective-permute-start.59
  63.7 1.6 collective-permute-start.18
  67.1 9.0 %collective-permute-done.59.refs_3_ = f32[8,2,64,128]{3,2,1,0:T(8,128)} collective-permute-done((f32[8,2,64,128]{3,2,1,0:T(8,128)}, f32[8,2,64,128]{3,2,1,0:T(8,128)}, u32[]{:S(2)}, u32[]{:S(2)}) %collective-permute-start.59) | collective-permute-done | bytes 524320 | tf_op jit(solution)/shard_map/ppermute | solution.py:237
  76.2 2.1 collective-permute-start.2
  78.3 2.1 collective-permute-done.17.refs_1_
  80.3 2.3 multiply_bitcast_fusion
  82.8 4.1 copy.34
  87.0 2.8 reshape.80.refs_4_
  89.8 4.3 shard_map.111
  94.1 2.9 collective-permute-start.60
  97.0 3.3 shard_map.109
  100.3 17.6 %collective-permute-done.19.refs_3_ = f32[8,2,64,128]{3,2,1,0:T(8,128)} collective-permute-done((f32[8,2,64,128]{3,2,1,0:T(8,128)}, f32[8,2,64,128]{3,2,1,0:T(8,128)}, u32[]{:S(2)}, u32[]{:S(2)}) %collective-permute-start.19) | collective-permute-done | bytes 524320 | tf_op jit(solution)/shard_map/ppermute | solution.py:237
  119.3 4.1 shard_map.106
  124.1 4.2 shard_map.104
  129.7 3.6 fusion.46
  134.5 3.5 collective-permute-start.61
  138.6 5.5 %collective-permute-done.43 = f32[4,16,2,16,128]{4,3,2,1,0:T(8,128)} collective-permute-done((f32[4,16,2,16,128]{4,3,2,1,0:T(8,128)}, f32[4,16,2,16,128]{4,3,2,1,0:T(8,128)}, u32[]{:S(2)}, u32[]{:S(2)}) %collective-permute-start.43) | collective-permute-done | bytes 1048608 | tf_op jit(solution)/shard_map/ppermute | solution.py:245
  145.3 3.4 collective-permute-start.44
  148.7 18.0 %collective-permute-done.20 = f32[4,16,2,16,128]{4,3,2,1,0:T(8,128)} collective-permute-done((f32[4,16,2,16,128]{4,3,2,1,0:T(8,128)}, f32[4,16,2,16,128]{4,3,2,1,0:T(8,128)}, u32[]{:S(2)}, u32[]{:S(2)}) %collective-permute-start.20) | collective-permute-done | bytes 1048608 | tf_op jit(solution)/shard_map/ppermute | solution.py:245
  168.4 20.5 %collective-permute-done.3 = f32[4,16,2,16,128]{4,3,2,1,0:T(8,128)} collective-permute-done((f32[4,16,2,16,128]{4,3,2,1,0:T(8,128)}, f32[4,16,2,16,128]{4,3,2,1,0:T(8,128)}, u32[]{:S(2)}, u32[]{:S(2)}) %collective-permute-start.3) | collective-permute-done | bytes 1048608 | tf_op jit(solution)/shard_map/ppermute | solution.py:245
  189.0 3.5 collective-permute-start.21
  199.2 4.4 collective-permute-start.62
  204.8 4.4 collective-permute-start.45
  210.9 3.9 collective-permute-start.22
  216.0 1.9 collective-permute-start.5
  217.9 3.5 collective-permute-start.63
  223.3 4.4 collective-permute-start.46
  229.6 5.2 collective-permute-start.23
  242.0 15.3 %collective-permute-start.6 = (f32[16,2,16,128]{3,2,1,0:T(8,128)S(1)}, f32[16,2,16,128]{3,2,1,0:T(8,128)S(1)}, u32[]{:S(2)}, u32[]{:S(2)}) collective-permute-start(f32[16,2,16,128]{3,2,1,0:T(8,128)S(1)} %get-tuple-element.113), channel_id=1, source_target_pairs={{0,8},{4,12},{8,16},{12,20},{16,24},{20,28},{1,9},{5,13},{9,17},{1... | collective-permute-start | bytes 786440 | tf_op jit(solution)/shard_map/ppermute | solution.py:251
  263.8 5.7 %collective-permute-done.49 = f32[16,2,16,128]{3,2,1,0:T(8,128)S(1)} collective-permute-done((f32[16,2,16,128]{3,2,1,0:T(8,128)S(1)}, f32[16,2,16,128]{3,2,1,0:T(8,128)S(1)}, u32[]{:S(2)}, u32[]{:S(2)}) %collective-permute-start.49) | collective-permute-done | bytes 262176 | tf_op jit(solution)/shard_map/ppermute | solution.py:251
  269.5 4.1 collective-permute-start.67
  275.2 4.4 collective-permute-start.68
  282.5 4.6 collective-permute-start.51
  290.0 4.6 collective-permute-start.28
  297.9 8.5 %collective-permute-start.11 = (f32[16,2,16,128]{3,2,1,0:T(8,128)S(1)}, f32[16,2,16,128]{3,2,1,0:T(8,128)S(1)}, u32[]{:S(2)}, u32[]{:S(2)}) collective-permute-start(f32[16,2,16,128]{3,2,1,0:T(8,128)S(1)} %fusion.31), channel_id=1, source_target_pairs={{0,8},{4,12},{8,16},{12,20},{16,24},{20,28},{1,9},{5,13},{9,17},{1... | collective-permute-start | bytes 786440 | tf_op jit(solution)/shard_map/ppermute | solution.py:251
  306.4 3.1 collective-permute-start.54
  309.5 6.4 %collective-permute-start.52 = (f32[16,2,16,128]{3,2,1,0:T(8,128)S(1)}, f32[16,2,16,128]{3,2,1,0:T(8,128)S(1)}, u32[]{:S(2)}, u32[]{:S(2)}) collective-permute-start(f32[16,2,16,128]{3,2,1,0:T(8,128)S(1)} %collective-permute-done.51), channel_id=1, source_target_pairs={{8,16},{12,20},{16,24},{20,28},{9,17},{13,21},{17,25},{21,29},{10,... | collective-permute-start | bytes 786440 | tf_op jit(solution)/shard_map/ppermute | solution.py:251
  317.3 7.2 %collective-permute-start.29 = (f32[16,2,16,128]{3,2,1,0:T(8,128)S(1)}, f32[16,2,16,128]{3,2,1,0:T(8,128)S(1)}, u32[]{:S(2)}, u32[]{:S(2)}) collective-permute-start(f32[16,2,16,128]{3,2,1,0:T(8,128)S(1)} %collective-permute-done.28), channel_id=1, source_target_pairs={{8,16},{12,20},{16,24},{20,28},{9,17},{13,21},{17,25},{21,29},{10,... | collective-permute-start | bytes 786440 | tf_op jit(solution)/shard_map/ppermute | solution.py:251
  330.0 6.1 %collective-permute-done.14 = f32[16,2,16,128]{3,2,1,0:T(8,128)S(1)} collective-permute-done((f32[16,2,16,128]{3,2,1,0:T(8,128)S(1)}, f32[16,2,16,128]{3,2,1,0:T(8,128)S(1)}, u32[]{:S(2)}, u32[]{:S(2)}) %collective-permute-start.14) | collective-permute-done | bytes 262176 | tf_op jit(solution)/shard_map/ppermute | solution.py:251
  338.1 3.6 collective-permute-done.72
  343.9 3.4 collective-permute-done.55
  349.7 3.2 collective-permute-done.32
  356.1 2.0 collective-permute-done.15
  359.9 2.7 reshape.83.refs_2_
  362.6 11.7 %collective-permute-done.73.refs_1_ = f32[4,16,2,16,128]{4,3,2,1,0:T(8,128)} collective-permute-done((f32[4,16,2,16,128]{4,3,2,1,0:T(8,128)S(1)}, f32[4,16,2,16,128]{4,3,2,1,0:T(8,128)}, u32[]{:S(2)}, u32[]{:S(2)}) %collective-permute-start.73) | collective-permute-done | bytes 1048608 | tf_op jit(solution)/shard_map/ppermute | solution.py:245
  374.3 4.1 shard_map.112
  384.1 12.7 %collective-permute-done.56.refs_1_ = f32[4,16,2,16,128]{4,3,2,1,0:T(8,128)} collective-permute-done((f32[4,16,2,16,128]{4,3,2,1,0:T(8,128)S(1)}, f32[4,16,2,16,128]{4,3,2,1,0:T(8,128)}, u32[]{:S(2)}, u32[]{:S(2)}) %collective-permute-start.56) | collective-permute-done | bytes 1048608 | tf_op jit(solution)/shard_map/ppermute | solution.py:245
  396.8 3.5 shard_map.110
  400.3 18.9 %collective-permute-done.33.refs_1_ = f32[4,16,2,16,128]{4,3,2,1,0:T(8,128)} collective-permute-done((f32[4,16,2,16,128]{4,3,2,1,0:T(8,128)}, f32[4,16,2,16,128]{4,3,2,1,0:T(8,128)}, u32[]{:S(2)}, u32[]{:S(2)}) %collective-permute-start.33) | collective-permute-done | bytes 1048608 | tf_op jit(solution)/shard_map/ppermute | solution.py:245
  419.3 3.5 shard_map.107
  422.8 17.1 %collective-permute-done.16.refs_1_ = f32[4,16,2,16,128]{4,3,2,1,0:T(8,128)} collective-permute-done((f32[4,16,2,16,128]{4,3,2,1,0:T(8,128)S(1)}, f32[4,16,2,16,128]{4,3,2,1,0:T(8,128)}, u32[]{:S(2)}, u32[]{:S(2)}) %collective-permute-start.16) | collective-permute-done | bytes 1048608 | tf_op jit(solution)/shard_map/ppermute | solution.py:245
  443.5 3.4 shard_map.105
  448.9 5.9 %collective-permute-done.76.refs_4_ = f32[8,2,64,128]{3,2,1,0:T(8,128)S(1)} collective-permute-done((f32[8,2,64,128]{3,2,1,0:T(8,128)S(1)}, f32[8,2,64,128]{3,2,1,0:T(8,128)S(1)}, u32[]{:S(2)}, u32[]{:S(2)}) %collective-permute-start.76) | collective-permute-done | bytes 524320 | tf_op jit(solution)/shard_map/ppermute | solution.py:237
  454.7 10.2 %collective-permute-done.78.refs_6_ = f32[8,2,64,128]{3,2,1,0:T(8,128)S(1)} collective-permute-done((f32[8,2,64,128]{3,2,1,0:T(8,128)S(1)}, f32[8,2,64,128]{3,2,1,0:T(8,128)S(1)}, u32[]{:S(2)}, u32[]{:S(2)}) %collective-permute-start.78) | collective-permute-done | bytes 524320 | tf_op jit(solution)/shard_map/ppermute | solution.py:237
  465.5 1.6 collective-permute-start.38
  468.6 19.9 %shard_map.113.refs_10_ = bf16[64,2,8,32,256]{4,3,2,1,0:T(8,128)(2,1)} custom-call(bf16[64,2,8,32,256]{4,3,2,1,0:T(8,128)(2,1)} %weight_ref.3, f32[8,2,64,128]{3,2,1,0:T(8,128)S(1)} %get-tuple-element.69.refs_0_, f32[8,2,64,128]{3,2,1,0:T(8,128)S(1)} %copy-done.5, f32[8,2,64,128]{3,2,1,0:T(8,128)S(1)} %collective-permute-done.74.refs_2_, ...), custom_call_target="tpu_custom_call" | custom-call | flops 4294967296 | bytes 20971520 | tf_op jit(solution)/shard_map/pallas_call | solution.py:188
  488.5 8.3 %collective-permute-done.36.refs_4_ = f32[8,2,64,128]{3,2,1,0:T(8,128)S(1)} collective-permute-done((f32[8,2,64,128]{3,2,1,0:T(8,128)S(1)}, f32[8,2,64,128]{3,2,1,0:T(8,128)S(1)}, u32[]{:S(2)}, u32[]{:S(2)}) %collective-permute-start.36) | collective-permute-done | bytes 524320 | tf_op jit(solution)/shard_map/ppermute | solution.py:237
  496.9 4.6 collective-permute-done.38.refs_6_
  501.5 19.9 %shard_map.114 = bf16[64,2,8,32,256]{4,3,2,1,0:T(8,128)(2,1)} custom-call(bf16[64,2,8,32,256]{4,3,2,1,0:T(8,128)(2,1)} %weight_ref.3, f32[8,2,64,128]{3,2,1,0:T(8,128)S(1)} %get-tuple-element.49.refs_0_, f32[8,2,64,128]{3,2,1,0:T(8,128)S(1)} %get-tuple-element.56.refs_1_, ...), custom_call_target="tpu_custom_call", output_to_operand_aliasing={{}: (11, {})} | custom-call | flops 4294967296 | bytes 20971520 | tf_op jit(solution)/shard_map/pallas_call | solution.py:188
  (248 shorter events, 87.9 us)
Async XLA Ops:
  24.4 37.4 %collective-permute-start.40 = (f32[8,2,64,128]{3,2,1,0:T(8,128)S(1)}, f32[8,2,64,128]{3,2,1,0:T(8,128)S(1)}, u32[]{:S(2)}, u32[]{:S(2)}) collective-permute-start(f32[8,2,64,128]{3,2,1,0:T(8,128)S(1)} %get-tuple-element.64), channel_id=1, source_target_pairs={{0,1},{1,2},{2,3},{3,0},{4,5},{5,6},{6,7},{7,4},{8,9},{9,10},{10,1... | collective-permute-start | bytes 1572872 | tf_op jit(solution)/shard_map/ppermute | solution.py:237
  24.8 38.6 %collective-permute-start.41 = (f32[8,2,64,128]{3,2,1,0:T(8,128)S(1)}, f32[8,2,64,128]{3,2,1,0:T(8,128)S(1)}, u32[]{:S(2)}, u32[]{:S(2)}) collective-permute-start(f32[8,2,64,128]{3,2,1,0:T(8,128)S(1)} %get-tuple-element.65), channel_id=1, source_target_pairs={{0,2},{1,3},{2,0},{3,1},{4,6},{5,7},{6,4},{7,5},{8,10},{9,11},{10,... | collective-permute-start | bytes 1572872 | tf_op jit(solution)/shard_map/ppermute | solution.py:237
  27.4 36.3 %collective-permute-start.42 = (f32[8,2,64,128]{3,2,1,0:T(8,128)}, f32[8,2,64,128]{3,2,1,0:T(8,128)S(1)}, u32[]{:S(2)}, u32[]{:S(2)}) collective-permute-start(f32[8,2,64,128]{3,2,1,0:T(8,128)} %get-tuple-element.66), channel_id=1, source_target_pairs={{0,3},{1,0},{2,1},{3,2},{4,7},{5,4},{6,5},{7,6},{8,11},{9,8},{10,9... | collective-permute-start | bytes 1572872 | tf_op jit(solution)/shard_map/ppermute | solution.py:237
  28.8 36.5 %collective-permute-start.57 = (f32[8,2,64,128]{3,2,1,0:T(8,128)}, f32[8,2,64,128]{3,2,1,0:T(8,128)}, u32[]{:S(2)}, u32[]{:S(2)}) collective-permute-start(f32[8,2,64,128]{3,2,1,0:T(8,128)} %get-tuple-element.71), channel_id=1, source_target_pairs={{0,1},{1,2},{2,3},{3,0},{4,5},{5,6},{6,7},{7,4},{8,9},{9,10},{10,1... | collective-permute-start | bytes 1572872 | tf_op jit(solution)/shard_map/ppermute | solution.py:237
  33.5 32.2 %collective-permute-start.58 = (f32[8,2,64,128]{3,2,1,0:T(8,128)}, f32[8,2,64,128]{3,2,1,0:T(8,128)}, u32[]{:S(2)}, u32[]{:S(2)}) collective-permute-start(f32[8,2,64,128]{3,2,1,0:T(8,128)} %get-tuple-element.72), channel_id=1, source_target_pairs={{0,2},{1,3},{2,0},{3,1},{4,6},{5,7},{6,4},{7,5},{8,10},{9,11},{10,... | collective-permute-start | bytes 1572872 | tf_op jit(solution)/shard_map/ppermute | solution.py:237
  61.8 14.4 %collective-permute-start.59 = (f32[8,2,64,128]{3,2,1,0:T(8,128)}, f32[8,2,64,128]{3,2,1,0:T(8,128)}, u32[]{:S(2)}, u32[]{:S(2)}) collective-permute-start(f32[8,2,64,128]{3,2,1,0:T(8,128)} %get-tuple-element.73), channel_id=1, source_target_pairs={{0,3},{1,0},{2,1},{3,2},{4,7},{5,4},{6,5},{7,6},{8,11},{9,8},{10,9... | collective-permute-start | bytes 1572872 | tf_op jit(solution)/shard_map/ppermute | solution.py:237
  63.5 16.8 %collective-permute-start.17 = (f32[8,2,64,128]{3,2,1,0:T(8,128)}, f32[8,2,64,128]{3,2,1,0:T(8,128)S(1)}, u32[]{:S(2)}, u32[]{:S(2)}) collective-permute-start(f32[8,2,64,128]{3,2,1,0:T(8,128)} %get-tuple-element.51), channel_id=1, source_target_pairs={{0,1},{1,2},{2,3},{3,0},{4,5},{5,6},{6,7},{7,4},{8,9},{9,10},{10,1... | collective-permute-start | bytes 1572872 | tf_op jit(solution)/shard_map/ppermute | solution.py:237
  63.7 30.4 %collective-permute-start.18 = (f32[8,2,64,128]{3,2,1,0:T(8,128)}, f32[8,2,64,128]{3,2,1,0:T(8,128)}, u32[]{:S(2)}, u32[]{:S(2)}) collective-permute-start(f32[8,2,64,128]{3,2,1,0:T(8,128)} %copy-done.16), channel_id=1, source_target_pairs={{0,2},{1,3},{2,0},{3,1},{4,6},{5,7},{6,4},{7,5},{8,10},{9,11},{10,... | collective-permute-start | bytes 1572872 | tf_op jit(solution)/shard_map/ppermute | solution.py:237
  65.3 58.1 %collective-permute-start = (f32[8,2,64,128]{3,2,1,0:T(8,128)}, f32[8,2,64,128]{3,2,1,0:T(8,128)}, u32[]{:S(2)}, u32[]{:S(2)}) collective-permute-start(f32[8,2,64,128]{3,2,1,0:T(8,128)} %copy-done.14), channel_id=1, source_target_pairs={{0,1},{1,2},{2,3},{3,0},{4,5},{5,6},{6,7},{7,4},{8,9},{9,10},{10,1... | collective-permute-start | bytes 1572872 | tf_op jit(solution)/shard_map/ppermute | solution.py:237
  65.7 58.4 %collective-permute-start.1 = (f32[8,2,64,128]{3,2,1,0:T(8,128)}, f32[8,2,64,128]{3,2,1,0:T(8,128)}, u32[]{:S(2)}, u32[]{:S(2)}) collective-permute-start(f32[8,2,64,128]{3,2,1,0:T(8,128)} %copy-done.13), channel_id=1, source_target_pairs={{0,2},{1,3},{2,0},{3,1},{4,6},{5,7},{6,4},{7,5},{8,10},{9,11},{10,... | collective-permute-start | bytes 1572872 | tf_op jit(solution)/shard_map/ppermute | solution.py:237
  76.2 47.9 %collective-permute-start.2 = (f32[8,2,64,128]{3,2,1,0:T(8,128)}, f32[8,2,64,128]{3,2,1,0:T(8,128)}, u32[]{:S(2)}, u32[]{:S(2)}) collective-permute-start(f32[8,2,64,128]{3,2,1,0:T(8,128)} %copy-done.12), channel_id=1, source_target_pairs={{0,3},{1,0},{2,1},{3,2},{4,7},{5,4},{6,5},{7,6},{8,11},{9,8},{10,9... | collective-permute-start | bytes 1572872 | tf_op jit(solution)/shard_map/ppermute | solution.py:237
  80.3 37.5 %collective-permute-start.19 = (f32[8,2,64,128]{3,2,1,0:T(8,128)}, f32[8,2,64,128]{3,2,1,0:T(8,128)}, u32[]{:S(2)}, u32[]{:S(2)}) collective-permute-start(f32[8,2,64,128]{3,2,1,0:T(8,128)} %copy-done.15), channel_id=1, source_target_pairs={{0,3},{1,0},{2,1},{3,2},{4,7},{5,4},{6,5},{7,6},{8,11},{9,8},{10,9... | collective-permute-start | bytes 1572872 | tf_op jit(solution)/shard_map/ppermute | solution.py:237
  94.1 39.2 %collective-permute-start.60 = (f32[4,16,2,16,128]{4,3,2,1,0:T(8,128)}, f32[4,16,2,16,128]{4,3,2,1,0:T(8,128)}, u32[]{:S(2)}, u32[]{:S(2)}) collective-permute-start(f32[4,16,2,16,128]{4,3,2,1,0:T(8,128)} %get-tuple-element.75), channel_id=1, source_target_pairs={{0,4},{4,0},{8,12},{12,8},{16,20},{20,16},{24,28},{28,24},{1,5},{5... | collective-permute-start | bytes 3145736 | tf_op jit(solution)/shard_map/ppermute | solution.py:245
  117.8 26.3 %collective-permute-start.43 = (f32[4,16,2,16,128]{4,3,2,1,0:T(8,128)}, f32[4,16,2,16,128]{4,3,2,1,0:T(8,128)}, u32[]{:S(2)}, u32[]{:S(2)}) collective-permute-start(f32[4,16,2,16,128]{4,3,2,1,0:T(8,128)} %get-tuple-element.68), channel_id=1, source_target_pairs={{0,4},{4,0},{8,12},{12,8},{16,20},{20,16},{24,28},{28,24},{1,5},{5... | collective-permute-start | bytes 3145736 | tf_op jit(solution)/shard_map/ppermute | solution.py:245
  123.5 43.2 %collective-permute-start.20 = (f32[4,16,2,16,128]{4,3,2,1,0:T(8,128)}, f32[4,16,2,16,128]{4,3,2,1,0:T(8,128)}, u32[]{:S(2)}, u32[]{:S(2)}) collective-permute-start(f32[4,16,2,16,128]{4,3,2,1,0:T(8,128)} %get-tuple-element.55), channel_id=1, source_target_pairs={{0,4},{4,0},{8,12},{12,8},{16,20},{20,16},{24,28},{28,24},{1,5},{5... | collective-permute-start | bytes 3145736 | tf_op jit(solution)/shard_map/ppermute | solution.py:245
  128.2 60.8 %collective-permute-start.3 = (f32[4,16,2,16,128]{4,3,2,1,0:T(8,128)}, f32[4,16,2,16,128]{4,3,2,1,0:T(8,128)}, u32[]{:S(2)}, u32[]{:S(2)}) collective-permute-start(f32[4,16,2,16,128]{4,3,2,1,0:T(8,128)} %get-tuple-element.48), channel_id=1, source_target_pairs={{0,4},{4,0},{8,12},{12,8},{16,20},{20,16},{24,28},{28,24},{1,5},{5... | collective-permute-start | bytes 3145736 | tf_op jit(solution)/shard_map/ppermute | solution.py:245
  134.5 59.2 %collective-permute-start.61 = (f32[16,2,16,128]{3,2,1,0:T(8,128)S(1)}, f32[16,2,16,128]{3,2,1,0:T(8,128)S(1)}, u32[]{:S(2)}, u32[]{:S(2)}) collective-permute-start(f32[16,2,16,128]{3,2,1,0:T(8,128)S(1)} %get-tuple-element.103), channel_id=1, source_target_pairs={{0,8},{4,12},{1,9},{5,13},{2,10},{6,14},{3,11},{7,15}} | collective-permute-start | bytes 786440 | tf_op jit(solution)/shard_map/ppermute | solution.py:251
  138.0 72.2 %collective-permute-start.64 = (f32[16,2,16,128]{3,2,1,0:T(8,128)S(1)}, f32[16,2,16,128]{3,2,1,0:T(8,128)S(1)}, u32[]{:S(2)}, u32[]{:S(2)}) collective-permute-start(f32[16,2,16,128]{3,2,1,0:T(8,128)S(1)} %get-tuple-element.104), channel_id=1, source_target_pairs={{24,16},{28,20},{25,17},{29,21},{26,18},{30,22},{27,19},{31,23}} | collective-permute-start | bytes 786440 | tf_op jit(solution)/shard_map/ppermute | solution.py:251
  145.3 50.1 %collective-permute-start.44 = (f32[16,2,16,128]{3,2,1,0:T(8,128)S(1)}, f32[16,2,16,128]{3,2,1,0:T(8,128)S(1)}, u32[]{:S(2)}, u32[]{:S(2)}) collective-permute-start(f32[16,2,16,128]{3,2,1,0:T(8,128)S(1)} %get-tuple-element.107), channel_id=1, source_target_pairs={{0,8},{4,12},{1,9},{5,13},{2,10},{6,14},{3,11},{7,15}} | collective-permute-start | bytes 786440 | tf_op jit(solution)/shard_map/ppermute | solution.py:251
  166.7 49.3 %collective-permute-start.47 = (f32[16,2,16,128]{3,2,1,0:T(8,128)S(1)}, f32[16,2,16,128]{3,2,1,0:T(8,128)S(1)}, u32[]{:S(2)}, u32[]{:S(2)}) collective-permute-start(f32[16,2,16,128]{3,2,1,0:T(8,128)S(1)} %get-tuple-element.108), channel_id=1, source_target_pairs={{24,16},{28,20},{25,17},{29,21},{26,18},{30,22},{27,19},{31,23}} | collective-permute-start | bytes 786440 | tf_op jit(solution)/shard_map/ppermute | solution.py:251
  193.6 29.0 %collective-permute-start.24 = (f32[16,2,16,128]{3,2,1,0:T(8,128)S(1)}, f32[16,2,16,128]{3,2,1,0:T(8,128)S(1)}, u32[]{:S(2)}, u32[]{:S(2)}) collective-permute-start(f32[16,2,16,128]{3,2,1,0:T(8,128)S(1)} %get-tuple-element.112), channel_id=1, source_target_pairs={{24,16},{28,20},{25,17},{29,21},{26,18},{30,22},{27,19},{31,23}} | collective-permute-start | bytes 786440 | tf_op jit(solution)/shard_map/ppermute | solution.py:251
  204.8 13.1 %collective-permute-start.45 = (f32[16,2,16,128]{3,2,1,0:T(8,128)S(1)}, f32[16,2,16,128]{3,2,1,0:T(8,128)S(1)}, u32[]{:S(2)}, u32[]{:S(2)}) collective-permute-start(f32[16,2,16,128]{3,2,1,0:T(8,128)S(1)} %bitcast_add_fusion.7), channel_id=1, source_target_pairs={{0,8},{4,12},{8,16},{12,20},{1,9},{5,13},{9,17},{13,21},{2,10},{6,... | collective-permute-start | bytes 786440 | tf_op jit(solution)/shard_map/ppermute | solution.py:251
  210.2 18.7 %collective-permute-start.7 = (f32[16,2,16,128]{3,2,1,0:T(8,128)S(1)}, f32[16,2,16,128]{3,2,1,0:T(8,128)S(1)}, u32[]{:S(2)}, u32[]{:S(2)}) collective-permute-start(f32[16,2,16,128]{3,2,1,0:T(8,128)S(1)} %get-tuple-element.116), channel_id=1, source_target_pairs={{24,16},{28,20},{25,17},{29,21},{26,18},{30,22},{27,19},{31,23}} | collective-permute-start | bytes 786440 | tf_op jit(solution)/shard_map/ppermute | solution.py:251
  216.0 13.6 %collective-permute-start.5 = (f32[16,2,16,128]{3,2,1,0:T(8,128)S(1)}, f32[16,2,16,128]{3,2,1,0:T(8,128)S(1)}, u32[]{:S(2)}, u32[]{:S(2)}) collective-permute-start(f32[16,2,16,128]{3,2,1,0:T(8,128)S(1)} %bitcast_add_fusion.17), channel_id=1, source_target_pairs={{0,8},{4,12},{8,16},{12,20},{1,9},{5,13},{9,17},{13,21},{2,10},{6,... | collective-permute-start | bytes 786440 | tf_op jit(solution)/shard_map/ppermute | solution.py:251
  217.9 40.4 %collective-permute-start.63 = (f32[16,2,16,128]{3,2,1,0:T(8,128)S(1)}, f32[16,2,16,128]{3,2,1,0:T(8,128)S(1)}, u32[]{:S(2)}, u32[]{:S(2)}) collective-permute-start(f32[16,2,16,128]{3,2,1,0:T(8,128)S(1)} %get-tuple-element.101), channel_id=1, source_target_pairs={{0,8},{4,12},{8,16},{12,20},{16,24},{20,28},{1,9},{5,13},{9,17},{1... | collective-permute-start | bytes 786440 | tf_op jit(solution)/shard_map/ppermute | solution.py:251
  222.6 13.4 %collective-permute-start.65 = (f32[16,2,16,128]{3,2,1,0:T(8,128)S(1)}, f32[16,2,16,128]{3,2,1,0:T(8,128)S(1)}, u32[]{:S(2)}, u32[]{:S(2)}) collective-permute-start(f32[16,2,16,128]{3,2,1,0:T(8,128)S(1)} %get-tuple-element.102), channel_id=1, source_target_pairs={{16,8},{20,12},{24,16},{28,20},{17,9},{21,13},{25,17},{29,21},{18,... | collective-permute-start | bytes 786440 | tf_op jit(solution)/shard_map/ppermute | solution.py:251
  223.3 39.2 %collective-permute-start.46 = (f32[16,2,16,128]{3,2,1,0:T(8,128)S(1)}, f32[16,2,16,128]{3,2,1,0:T(8,128)S(1)}, u32[]{:S(2)}, u32[]{:S(2)}) collective-permute-start(f32[16,2,16,128]{3,2,1,0:T(8,128)S(1)} %get-tuple-element.105), channel_id=1, source_target_pairs={{0,8},{4,12},{8,16},{12,20},{16,24},{20,28},{1,9},{5,13},{9,17},{1... | collective-permute-start | bytes 786440 | tf_op jit(solution)/shard_map/ppermute | solution.py:251
  229.6 45.5 %collective-permute-start.23 = (f32[16,2,16,128]{3,2,1,0:T(8,128)S(1)}, f32[16,2,16,128]{3,2,1,0:T(8,128)S(1)}, u32[]{:S(2)}, u32[]{:S(2)}) collective-permute-start(f32[16,2,16,128]{3,2,1,0:T(8,128)S(1)} %get-tuple-element.109), channel_id=1, source_target_pairs={{0,8},{4,12},{8,16},{12,20},{16,24},{20,28},{1,9},{5,13},{9,17},{1... | collective-permute-start | bytes 786440 | tf_op jit(solution)/shard_map/ppermute | solution.py:251
  239.4 20.2 %collective-permute-start.66 = (f32[16,2,16,128]{3,2,1,0:T(8,128)S(1)}, f32[16,2,16,128]{3,2,1,0:T(8,128)S(1)}, u32[]{:S(2)}, u32[]{:S(2)}) collective-permute-start(f32[16,2,16,128]{3,2,1,0:T(8,128)S(1)} %bitcast_add_fusion.1), channel_id=1, source_target_pairs={{8,0},{12,4},{16,8},{20,12},{24,16},{28,20},{9,1},{13,5},{17,9},{2... | collective-permute-start | bytes 786440 | tf_op jit(solution)/shard_map/ppermute | solution.py:251
  242.0 40.5 %collective-permute-start.6 = (f32[16,2,16,128]{3,2,1,0:T(8,128)S(1)}, f32[16,2,16,128]{3,2,1,0:T(8,128)S(1)}, u32[]{:S(2)}, u32[]{:S(2)}) collective-permute-start(f32[16,2,16,128]{3,2,1,0:T(8,128)S(1)} %get-tuple-element.113), channel_id=1, source_target_pairs={{0,8},{4,12},{8,16},{12,20},{16,24},{20,28},{1,9},{5,13},{9,17},{1... | collective-permute-start | bytes 786440 | tf_op jit(solution)/shard_map/ppermute | solution.py:251
  259.7 20.0 %collective-permute-start.26 = (f32[16,2,16,128]{3,2,1,0:T(8,128)S(1)}, f32[16,2,16,128]{3,2,1,0:T(8,128)S(1)}, u32[]{:S(2)}, u32[]{:S(2)}) collective-permute-start(f32[16,2,16,128]{3,2,1,0:T(8,128)S(1)} %bitcast_add_fusion.11), channel_id=1, source_target_pairs={{8,0},{12,4},{16,8},{20,12},{24,16},{28,20},{9,1},{13,5},{17,9},{2... | collective-permute-start | bytes 786440 | tf_op jit(solution)/shard_map/ppermute | solution.py:251
  262.5 24.6 %collective-permute-start.9 = (f32[16,2,16,128]{3,2,1,0:T(8,128)S(1)}, f32[16,2,16,128]{3,2,1,0:T(8,128)S(1)}, u32[]{:S(2)}, u32[]{:S(2)}) collective-permute-start(f32[16,2,16,128]{3,2,1,0:T(8,128)S(1)} %bitcast_add_fusion.16), channel_id=1, source_target_pairs={{8,0},{12,4},{16,8},{20,12},{24,16},{28,20},{9,1},{13,5},{17,9},{2... | collective-permute-start | bytes 786440 | tf_op jit(solution)/shard_map/ppermute | solution.py:251
  269.5 20.5 %collective-permute-start.67 = (f32[16,2,16,128]{3,2,1,0:T(8,128)S(1)}, f32[16,2,16,128]{3,2,1,0:T(8,128)S(1)}, u32[]{:S(2)}, u32[]{:S(2)}) collective-permute-start(f32[16,2,16,128]{3,2,1,0:T(8,128)S(1)} %fusion.37), channel_id=1, source_target_pairs={{8,0},{12,4},{16,8},{20,12},{24,16},{28,20},{9,1},{13,5},{17,9},{2... | collective-permute-start | bytes 786440 | tf_op jit(solution)/shard_map/ppermute | solution.py:251
  275.2 19.4 %collective-permute-start.68 = (f32[16,2,16,128]{3,2,1,0:T(8,128)S(1)}, f32[16,2,16,128]{3,2,1,0:T(8,128)S(1)}, u32[]{:S(2)}, u32[]{:S(2)}) collective-permute-start(f32[16,2,16,128]{3,2,1,0:T(8,128)S(1)} %fusion.37), channel_id=1, source_target_pairs={{0,8},{4,12},{8,16},{12,20},{16,24},{20,28},{1,9},{5,13},{9,17},{1... | collective-permute-start | bytes 786440 | tf_op jit(solution)/shard_map/ppermute | solution.py:251
  279.6 16.3 %collective-permute-start.50 = (f32[16,2,16,128]{3,2,1,0:T(8,128)S(1)}, f32[16,2,16,128]{3,2,1,0:T(8,128)S(1)}, u32[]{:S(2)}, u32[]{:S(2)}) collective-permute-start(f32[16,2,16,128]{3,2,1,0:T(8,128)S(1)} %fusion.35), channel_id=1, source_target_pairs={{8,0},{12,4},{16,8},{20,12},{24,16},{28,20},{9,1},{13,5},{17,9},{2... | collective-permute-start | bytes 786440 | tf_op jit(solution)/shard_map/ppermute | solution.py:251
  282.5 14.7 %collective-permute-start.51 = (f32[16,2,16,128]{3,2,1,0:T(8,128)S(1)}, f32[16,2,16,128]{3,2,1,0:T(8,128)S(1)}, u32[]{:S(2)}, u32[]{:S(2)}) collective-permute-start(f32[16,2,16,128]{3,2,1,0:T(8,128)S(1)} %fusion.35), channel_id=1, source_target_pairs={{0,8},{4,12},{8,16},{12,20},{16,24},{20,28},{1,9},{5,13},{9,17},{1... | collective-permute-start | bytes 786440 | tf_op jit(solution)/shard_map/ppermute | solution.py:251
  290.0 16.4 %collective-permute-start.28 = (f32[16,2,16,128]{3,2,1,0:T(8,128)S(1)}, f32[16,2,16,128]{3,2,1,0:T(8,128)S(1)}, u32[]{:S(2)}, u32[]{:S(2)}) collective-permute-start(f32[16,2,16,128]{3,2,1,0:T(8,128)S(1)} %fusion.33), channel_id=1, source_target_pairs={{0,8},{4,12},{8,16},{12,20},{16,24},{20,28},{1,9},{5,13},{9,17},{1... | collective-permute-start | bytes 786440 | tf_op jit(solution)/shard_map/ppermute | solution.py:251
  294.6 15.0 %collective-permute-start.10 = (f32[16,2,16,128]{3,2,1,0:T(8,128)S(1)}, f32[16,2,16,128]{3,2,1,0:T(8,128)S(1)}, u32[]{:S(2)}, u32[]{:S(2)}) collective-permute-start(f32[16,2,16,128]{3,2,1,0:T(8,128)S(1)} %fusion.31), channel_id=1, source_target_pairs={{8,0},{12,4},{16,8},{20,12},{24,16},{28,20},{9,1},{13,5},{17,9},{2... | collective-permute-start | bytes 786440 | tf_op jit(solution)/shard_map/ppermute | solution.py:251
  295.9 20.1 %collective-permute-start.71 = (f32[16,2,16,128]{3,2,1,0:T(8,128)S(1)}, f32[16,2,16,128]{3,2,1,0:T(8,128)S(1)}, u32[]{:S(2)}, u32[]{:S(2)}) collective-permute-start(f32[16,2,16,128]{3,2,1,0:T(8,128)S(1)} %collective-permute-done.67), channel_id=1, source_target_pairs={{8,0},{12,4},{16,8},{20,12},{9,1},{13,5},{17,9},{21,13},{10,2},{14... | collective-permute-start | bytes 786440 | tf_op jit(solution)/shard_map/ppermute | solution.py:251
  297.2 20.1 %collective-permute-start.69 = (f32[16,2,16,128]{3,2,1,0:T(8,128)S(1)}, f32[16,2,16,128]{3,2,1,0:T(8,128)S(1)}, u32[]{:S(2)}, u32[]{:S(2)}) collective-permute-start(f32[16,2,16,128]{3,2,1,0:T(8,128)S(1)} %collective-permute-done.68), channel_id=1, source_target_pairs={{8,16},{12,20},{16,24},{20,28},{9,17},{13,21},{17,25},{21,29},{10,... | collective-permute-start | bytes 786440 | tf_op jit(solution)/shard_map/ppermute | solution.py:251
  297.9 26.7 %collective-permute-start.11 = (f32[16,2,16,128]{3,2,1,0:T(8,128)S(1)}, f32[16,2,16,128]{3,2,1,0:T(8,128)S(1)}, u32[]{:S(2)}, u32[]{:S(2)}) collective-permute-start(f32[16,2,16,128]{3,2,1,0:T(8,128)S(1)} %fusion.31), channel_id=1, source_target_pairs={{0,8},{4,12},{8,16},{12,20},{16,24},{20,28},{1,9},{5,13},{9,17},{1... | collective-permute-start | bytes 786440 | tf_op jit(solution)/shard_map/ppermute | solution.py:251
  306.4 19.5 %collective-permute-start.54 = (f32[16,2,16,128]{3,2,1,0:T(8,128)S(1)}, f32[16,2,16,128]{3,2,1,0:T(8,128)S(1)}, u32[]{:S(2)}, u32[]{:S(2)}) collective-permute-start(f32[16,2,16,128]{3,2,1,0:T(8,128)S(1)} %collective-permute-done.50), channel_id=1, source_target_pairs={{8,0},{12,4},{16,8},{20,12},{9,1},{13,5},{17,9},{21,13},{10,2},{14... | collective-permute-start | bytes 786440 | tf_op jit(solution)/shard_map/ppermute | solution.py:251
  309.5 17.0 %collective-permute-start.52 = (f32[16,2,16,128]{3,2,1,0:T(8,128)S(1)}, f32[16,2,16,128]{3,2,1,0:T(8,128)S(1)}, u32[]{:S(2)}, u32[]{:S(2)}) collective-permute-start(f32[16,2,16,128]{3,2,1,0:T(8,128)S(1)} %collective-permute-done.51), channel_id=1, source_target_pairs={{8,16},{12,20},{16,24},{20,28},{9,17},{13,21},{17,25},{21,29},{10,... | collective-permute-start | bytes 786440 | tf_op jit(solution)/shard_map/ppermute | solution.py:251
  326.6 15.1 %collective-permute-start.72 = (f32[16,2,16,128]{3,2,1,0:T(8,128)S(1)}, f32[16,2,16,128]{3,2,1,0:T(8,128)S(1)}, u32[]{:S(2)}, u32[]{:S(2)}) collective-permute-start(f32[16,2,16,128]{3,2,1,0:T(8,128)S(1)} %collective-permute-done.71), channel_id=1, source_target_pairs={{8,0},{12,4},{9,1},{13,5},{10,2},{14,6},{11,3},{15,7}} | collective-permute-start | bytes 786440 | tf_op jit(solution)/shard_map/ppermute | solution.py:251
  327.9 14.5 %collective-permute-start.70 = (f32[16,2,16,128]{3,2,1,0:T(8,128)S(1)}, f32[16,2,16,128]{3,2,1,0:T(8,128)S(1)}, u32[]{:S(2)}, u32[]{:S(2)}) collective-permute-start(f32[16,2,16,128]{3,2,1,0:T(8,128)S(1)} %collective-permute-done.69), channel_id=1, source_target_pairs={{16,24},{20,28},{17,25},{21,29},{18,26},{22,30},{19,27},{23,31}} | collective-permute-start | bytes 786440 | tf_op jit(solution)/shard_map/ppermute | solution.py:251
  328.6 18.7 %collective-permute-start.55 = (f32[16,2,16,128]{3,2,1,0:T(8,128)S(1)}, f32[16,2,16,128]{3,2,1,0:T(8,128)S(1)}, u32[]{:S(2)}, u32[]{:S(2)}) collective-permute-start(f32[16,2,16,128]{3,2,1,0:T(8,128)S(1)} %collective-permute-done.54), channel_id=1, source_target_pairs={{8,0},{12,4},{9,1},{13,5},{10,2},{14,6},{11,3},{15,7}} | collective-permute-start | bytes 786440 | tf_op jit(solution)/shard_map/ppermute | solution.py:251
  336.8 16.2 %collective-permute-start.32 = (f32[16,2,16,128]{3,2,1,0:T(8,128)S(1)}, f32[16,2,16,128]{3,2,1,0:T(8,128)S(1)}, u32[]{:S(2)}, u32[]{:S(2)}) collective-permute-start(f32[16,2,16,128]{3,2,1,0:T(8,128)S(1)} %collective-permute-done.31), channel_id=1, source_target_pairs={{8,0},{12,4},{9,1},{13,5},{10,2},{14,6},{11,3},{15,7}} | collective-permute-start | bytes 786440 | tf_op jit(solution)/shard_map/ppermute | solution.py:251
  342.4 15.6 %collective-permute-start.15 = (f32[16,2,16,128]{3,2,1,0:T(8,128)S(1)}, f32[16,2,16,128]{3,2,1,0:T(8,128)S(1)}, u32[]{:S(2)}, u32[]{:S(2)}) collective-permute-start(f32[16,2,16,128]{3,2,1,0:T(8,128)S(1)} %collective-permute-done.14), channel_id=1, source_target_pairs={{8,0},{12,4},{9,1},{13,5},{10,2},{14,6},{11,3},{15,7}} | collective-permute-start | bytes 786440 | tf_op jit(solution)/shard_map/ppermute | solution.py:251
  348.0 26.3 %collective-permute-start.73 = (f32[4,16,2,16,128]{4,3,2,1,0:T(8,128)S(1)}, f32[4,16,2,16,128]{4,3,2,1,0:T(8,128)}, u32[]{:S(2)}, u32[]{:S(2)}) collective-permute-start(f32[4,16,2,16,128]{4,3,2,1,0:T(8,128)S(1)} %pad_maximum_fusion.3.refs_0_), channel_id=1, source_target_pairs={{0,4},{4,0},{8,12},{12,8},{16,20},{20,16},{24,28},{28,24},{1,5},{5... | collective-permute-start | bytes 3145736 | tf_op jit(solution)/shard_map/ppermute | solution.py:245
  352.9 43.8 %collective-permute-start.56 = (f32[4,16,2,16,128]{4,3,2,1,0:T(8,128)S(1)}, f32[4,16,2,16,128]{4,3,2,1,0:T(8,128)}, u32[]{:S(2)}, u32[]{:S(2)}) collective-permute-start(f32[4,16,2,16,128]{4,3,2,1,0:T(8,128)S(1)} %pad_maximum_fusion.2.refs_0_), channel_id=1, source_target_pairs={{0,4},{4,0},{8,12},{12,8},{16,20},{20,16},{24,28},{28,24},{1,5},{5... | collective-permute-start | bytes 3145736 | tf_op jit(solution)/shard_map/ppermute | solution.py:245
  355.5 63.7 %collective-permute-start.33 = (f32[4,16,2,16,128]{4,3,2,1,0:T(8,128)}, f32[4,16,2,16,128]{4,3,2,1,0:T(8,128)}, u32[]{:S(2)}, u32[]{:S(2)}) collective-permute-start(f32[4,16,2,16,128]{4,3,2,1,0:T(8,128)} %pad_maximum_fusion.1.refs_0_), channel_id=1, source_target_pairs={{0,4},{4,0},{8,12},{12,8},{16,20},{20,16},{24,28},{28,24},{1,5},{5... | collective-permute-start | bytes 3145736 | tf_op jit(solution)/shard_map/ppermute | solution.py:245
  358.2 81.6 %collective-permute-start.16 = (f32[4,16,2,16,128]{4,3,2,1,0:T(8,128)S(1)}, f32[4,16,2,16,128]{4,3,2,1,0:T(8,128)}, u32[]{:S(2)}, u32[]{:S(2)}) collective-permute-start(f32[4,16,2,16,128]{4,3,2,1,0:T(8,128)S(1)} %pad_maximum_fusion.refs_0_), channel_id=1, source_target_pairs={{0,4},{4,0},{8,12},{12,8},{16,20},{20,16},{24,28},{28,24},{1,5},{5... | collective-permute-start | bytes 3145736 | tf_op jit(solution)/shard_map/ppermute | solution.py:245
  380.1 61.3 %collective-permute-start.75 = (f32[8,2,64,128]{3,2,1,0:T(8,128)}, f32[8,2,64,128]{3,2,1,0:T(8,128)S(1)}, u32[]{:S(2)}, u32[]{:S(2)}) collective-permute-start(f32[8,2,64,128]{3,2,1,0:T(8,128)} %get-tuple-element.78), channel_id=1, source_target_pairs={{0,1},{1,2},{2,3},{3,0},{4,5},{5,6},{6,7},{7,4},{8,9},{9,10},{10,1... | collective-permute-start | bytes 1572872 | tf_op jit(solution)/shard_map/ppermute | solution.py:237
  380.1 61.3 %collective-permute-start.77 = (f32[8,2,64,128]{3,2,1,0:T(8,128)}, f32[8,2,64,128]{3,2,1,0:T(8,128)}, u32[]{:S(2)}, u32[]{:S(2)}) collective-permute-start(f32[8,2,64,128]{3,2,1,0:T(8,128)} %get-tuple-element.80), channel_id=1, source_target_pairs={{0,2},{1,3},{2,0},{3,1},{4,6},{5,7},{6,4},{7,5},{8,10},{9,11},{10,... | collective-permute-start | bytes 1572872 | tf_op jit(solution)/shard_map/ppermute | solution.py:237
  396.8 50.2 %collective-permute-start.79 = (f32[8,2,64,128]{3,2,1,0:T(8,128)}, f32[8,2,64,128]{3,2,1,0:T(8,128)S(1)}, u32[]{:S(2)}, u32[]{:S(2)}) collective-permute-start(f32[8,2,64,128]{3,2,1,0:T(8,128)} %copy-done.17), channel_id=1, source_target_pairs={{0,3},{1,0},{2,1},{3,2},{4,7},{5,4},{6,5},{7,6},{8,11},{9,8},{10,9... | collective-permute-start | bytes 1572872 | tf_op jit(solution)/shard_map/ppermute | solution.py:237
  419.2 28.3 %collective-permute-start.74 = (f32[8,2,64,128]{3,2,1,0:T(8,128)S(1)}, f32[8,2,64,128]{3,2,1,0:T(8,128)S(1)}, u32[]{:S(2)}, u32[]{:S(2)}) collective-permute-start(f32[8,2,64,128]{3,2,1,0:T(8,128)S(1)} %get-tuple-element.77), channel_id=1, source_target_pairs={{0,1},{1,2},{2,3},{3,0},{4,5},{5,6},{6,7},{7,4},{8,9},{9,10},{10,1... | collective-permute-start | bytes 1572872 | tf_op jit(solution)/shard_map/ppermute | solution.py:237
  439.9 14.9 %collective-permute-start.76 = (f32[8,2,64,128]{3,2,1,0:T(8,128)S(1)}, f32[8,2,64,128]{3,2,1,0:T(8,128)S(1)}, u32[]{:S(2)}, u32[]{:S(2)}) collective-permute-start(f32[8,2,64,128]{3,2,1,0:T(8,128)S(1)} %get-tuple-element.79), channel_id=1, source_target_pairs={{0,2},{1,3},{2,0},{3,1},{4,6},{5,7},{6,4},{7,5},{8,10},{9,11},{10,... | collective-permute-start | bytes 1572872 | tf_op jit(solution)/shard_map/ppermute | solution.py:237
  441.3 23.6 %collective-permute-start.78 = (f32[8,2,64,128]{3,2,1,0:T(8,128)S(1)}, f32[8,2,64,128]{3,2,1,0:T(8,128)S(1)}, u32[]{:S(2)}, u32[]{:S(2)}) collective-permute-start(f32[8,2,64,128]{3,2,1,0:T(8,128)S(1)} %get-tuple-element.81), channel_id=1, source_target_pairs={{0,3},{1,0},{2,1},{3,2},{4,7},{5,4},{6,5},{7,6},{8,11},{9,8},{10,9... | collective-permute-start | bytes 1572872 | tf_op jit(solution)/shard_map/ppermute | solution.py:237
  441.3 24.2 %collective-permute-start.35 = (f32[8,2,64,128]{3,2,1,0:T(8,128)S(1)}, f32[8,2,64,128]{3,2,1,0:T(8,128)S(1)}, u32[]{:S(2)}, u32[]{:S(2)}) collective-permute-start(f32[8,2,64,128]{3,2,1,0:T(8,128)S(1)} %get-tuple-element.58), channel_id=1, source_target_pairs={{0,1},{1,2},{2,3},{3,0},{4,5},{5,6},{6,7},{7,4},{8,9},{9,10},{10,1... | collective-permute-start | bytes 1572872 | tf_op jit(solution)/shard_map/ppermute | solution.py:237
  447.0 41.6 %collective-permute-start.37 = (f32[8,2,64,128]{3,2,1,0:T(8,128)S(1)}, f32[8,2,64,128]{3,2,1,0:T(8,128)S(1)}, u32[]{:S(2)}, u32[]{:S(2)}) collective-permute-start(f32[8,2,64,128]{3,2,1,0:T(8,128)S(1)} %get-tuple-element.60), channel_id=1, source_target_pairs={{0,2},{1,3},{2,0},{3,1},{4,6},{5,7},{6,4},{7,5},{8,10},{9,11},{10,... | collective-permute-start | bytes 1572872 | tf_op jit(solution)/shard_map/ppermute | solution.py:237
  447.6 40.9 %collective-permute-start.39 = (f32[8,2,64,128]{3,2,1,0:T(8,128)S(1)}, f32[8,2,64,128]{3,2,1,0:T(8,128)S(1)}, u32[]{:S(2)}, u32[]{:S(2)}) collective-permute-start(f32[8,2,64,128]{3,2,1,0:T(8,128)S(1)} %get-tuple-element.62), channel_id=1, source_target_pairs={{0,3},{1,0},{2,1},{3,2},{4,7},{5,4},{6,5},{7,6},{8,11},{9,8},{10,9... | collective-permute-start | bytes 1572872 | tf_op jit(solution)/shard_map/ppermute | solution.py:237
  454.7 33.8 %collective-permute-start.34 = (f32[8,2,64,128]{3,2,1,0:T(8,128)S(1)}, f32[8,2,64,128]{3,2,1,0:T(8,128)S(1)}, u32[]{:S(2)}, u32[]{:S(2)}) collective-permute-start(f32[8,2,64,128]{3,2,1,0:T(8,128)S(1)} %get-tuple-element.57), channel_id=1, source_target_pairs={{0,1},{1,2},{2,3},{3,0},{4,5},{5,6},{6,7},{7,4},{8,9},{9,10},{10,1... | collective-permute-start | bytes 1572872 | tf_op jit(solution)/shard_map/ppermute | solution.py:237
  464.9 31.9 %collective-permute-start.36 = (f32[8,2,64,128]{3,2,1,0:T(8,128)S(1)}, f32[8,2,64,128]{3,2,1,0:T(8,128)S(1)}, u32[]{:S(2)}, u32[]{:S(2)}) collective-permute-start(f32[8,2,64,128]{3,2,1,0:T(8,128)S(1)} %get-tuple-element.59), channel_id=1, source_target_pairs={{0,2},{1,3},{2,0},{3,1},{4,6},{5,7},{6,4},{7,5},{8,10},{9,11},{10,... | collective-permute-start | bytes 1572872 | tf_op jit(solution)/shard_map/ppermute | solution.py:237
  465.5 36.0 %collective-permute-start.38 = (f32[8,2,64,128]{3,2,1,0:T(8,128)S(1)}, f32[8,2,64,128]{3,2,1,0:T(8,128)S(1)}, u32[]{:S(2)}, u32[]{:S(2)}) collective-permute-start(f32[8,2,64,128]{3,2,1,0:T(8,128)S(1)} %get-tuple-element.61), channel_id=1, source_target_pairs={{0,3},{1,0},{2,1},{3,2},{4,7},{5,4},{6,5},{7,6},{8,11},{9,8},{10,9... | collective-permute-start | bytes 1572872 | tf_op jit(solution)/shard_map/ppermute | solution.py:237
  (50 other events, 691.2 us)

commit v2 on v1

--- a/solution.py
+++ b/solution.py
@@ -61,12 +61,15 @@
     each = ranks // groups
 
     def body(grad_ref, factor_ref, select_ref, *outs):
-        matrix = split(select_ref[...])
+        matrix = jnp.concatenate(split(select_ref[...]), axis=0)
+        count = select_ref.shape[0]
         factor = factor_ref[...]
         for block in range(ins // ROWS):
             rows = pl.ds(block * ROWS, ROWS)
             lines = grad_ref[rows, 0, 0].reshape(ROWS * modes_b, out_ch)
-            done = dot3(matrix, dot(lines, factor)).reshape(modes, groups, each, ROWS, rank_out)
+            both = dot(matrix, lines)
+            both = dot(jnp.concatenate(split(both[:count] + both[count:]), axis=0), factor)
+            done = (both[:count] + both[count:]).reshape(modes, groups, each, ROWS, rank_out)
             for peer in range(modes):
                 for group in range(groups):
                     outs[peer * groups + group][0, :, rows, :] = done[peer, group]
@@ -250,9 +253,7 @@
         ]
         return lax.ppermute(value, "chan", pairs)
 
-    def scatter(held):
-        arrived = [held[0]] + [to_across(held[d], d) for d in range(1, across)]
-
+    def scatter(arrived):
         def local(q):
             q = jnp.clip(q, 0, along - 1)
             terms = [lax.dynamic_index_in_dim(v, q, 0, keepdims=False) for v in arrived]
@@ -279,45 +280,71 @@
             rights.append(right)
             lefts.append(left)
         slots = [value] + [lefts[j - 1] + rights[last - j] for j in range(1, along)]
-        full = jnp.stack(slots)
-        return [full] + [to_across(full, d) for d in range(1, across)]
-
-    shares = {}
+        return jnp.stack(slots)
+
+    each = ranks // groups
+    chunks = [(p, g) for p in range(parts) for g in range(groups)]
+    narrowed = {}
     for p in range(parts):
-        narrowed = narrow(gradient, u_out, narrow_b, p, modes, groups)
-        for g in range(groups):
-            pieces = [to_mode(narrowed[d * groups + g], d) for d in range(modes)]
-            held = gather_core(pieces, narrow_a, forward_columns, rank_a, across, along)
-            shares[p, g] = scatter(held)
-
-    wides, firsts, seconds = {}, [], []
-    each = ranks // groups
-    for p in range(parts):
-        first_parts, second_parts = [], []
-        for g in range(groups):
-            core = shares[p, g].transpose(2, 0, 1, 3)
-            old_first = first_moment[:, p, :, g * each : (g + 1) * each]
-            old_second = second_moment[:, p, :, g * each : (g + 1) * each]
-            new_first = BETA_ONE * old_first + (1.0 - BETA_ONE) * core
-            new_second = BETA_TWO * old_second + (1.0 - BETA_TWO) * core * core
-            direction = (
-                new_first
-                / (1.0 - BETA_ONE**STEP)
-                / (jnp.sqrt(new_second / (1.0 - BETA_TWO**STEP)) + 1e-08)
-            )
-            first_parts.append(new_first)
-            second_parts.append(new_second)
-            pieces = gather(direction.transpose(1, 2, 0, 3))
-            outs = spread_back(pieces, widen_a, backward_columns, modes)
-            for d in range(modes):
-                wides[p, d, g] = to_mode(outs[d], d)
-        firsts.append(jnp.concatenate(first_parts, axis=2))
-        seconds.append(jnp.concatenate(second_parts, axis=2))
+        chosen = narrow_b
+        if p > 0:
+            chosen = lax.optimization_barrier((narrow_b, narrowed[p - 1]))[0]
+        narrowed[p] = narrow(gradient, u_out, chosen, p, modes, groups)
+    moments = {}
+
+    def send_narrowed(key, pieces):
+        return [to_mode(v, d) for d, v in enumerate(pieces)]
+
+    def send_across(key, pieces):
+        held = gather_core(pieces, narrow_a, forward_columns, rank_a, across, along)
+        return [held[0]] + [to_across(held[d], d) for d in range(1, across)]
+
+    def sum_along(key, arrived):
+        return [scatter(arrived)]
+
+    def step(key, state):
+        p, g = key
+        core = state[0].transpose(2, 0, 1, 3)
+        old_first = first_moment[:, p, :, g * each : (g + 1) * each]
+        old_second = second_moment[:, p, :, g * each : (g + 1) * each]
+        new_first = BETA_ONE * old_first + (1.0 - BETA_ONE) * core
+        new_second = BETA_TWO * old_second + (1.0 - BETA_TWO) * core * core
+        direction = (
+            new_first
+            / (1.0 - BETA_ONE**STEP)
+            / (jnp.sqrt(new_second / (1.0 - BETA_TWO**STEP)) + 1e-08)
+        )
+        moments[key] = (new_first, new_second)
+        return [gather(direction.transpose(1, 2, 0, 3))]
+
+    def share_across(key, state):
+        return state + [to_across(state[0], d) for d in range(1, across)]
+
+    def send_wide(key, pieces):
+        outs = spread_back(pieces, widen_a, backward_columns, modes)
+        return [to_mode(v, d) for d, v in enumerate(outs)]
+
+    stages = [send_narrowed, send_across, sum_along, step, share_across, send_wide]
+    states = [[narrowed[p][d * groups + g] for d in range(modes)] for p, g in chunks]
+    for tick in range(len(chunks) + len(stages) - 1):
+        active = [c for c in range(len(chunks)) if 0 <= tick - c < len(stages)]
+        for c in active:
+            states[c] = stages[tick - c](chunks[c], states[c])
+        if tick + 1 < len(chunks):
+            active = active + [tick + 1]
+        held = lax.optimization_barrier([states[c] for c in active])
+        for c, value in zip(active, held):
+            states[c] = value
+    wides = {(*chunks[c], d): states[c][d] for c in range(len(chunks)) for d in range(modes)}
+    firsts, seconds = (
+        [jnp.concatenate([moments[p, g][m] for g in range(groups)], axis=2) for p in range(parts)]
+        for m in range(2)
+    )
 
     new_weight = None
     back = u_out.T
     for p in range(parts):
-        pieces = [wides[p, d, g] for d in range(modes) for g in range(groups)]
+        pieces = [wides[p, g, d] for d in range(modes) for g in range(groups)]
         new_weight = update(weight, pieces, back, widen_b, new_weight, p, groups)
     return (new_weight, jnp.stack(firsts, axis=1), jnp.stack(seconds, axis=1))
 

time: 525 us -> 446 us (0.85)
  starting transfers between devices: 167 us -> 126 us
  Pallas kernels: 111 us -> 84.1 us
  waiting for transfers between devices: 188 us -> 168 us
  local copies, waits for them, and re-layouts: 23.5 us -> 35.9 us
    ppermute x8, waiting for transfers between devices: 104 us -> 11.1 us  [to_across(): return lax.ppermute(value, 'chan', pairs)]
    ppermute x48, waiting for transfers between devices: 25.8 us -> 85.5 us  [to_along(): return lax.ppermute(value, 'chan', pairs)]
    ppermute x48, starting transfers between devices: 125 us -> 97.6 us  [to_along(): return lax.ppermute(value, 'chan', pairs)]
    pallas_call x2, Pallas kernels: 40.4 us -> 21.1 us  [narrow(): call(body, (local_a,), [pl.BlockSpec((ins, 1, 1, modes_b, out_ch), lambda...]
    ppermute x24, waiting for transfers between devices: 57.7 us -> 71.9 us  [to_mode(): lax.ppermute(value, 'mode', [(m, (m + d) % modes) for m in range(modes)])]
    unnamed x73 -> x135, local copies, waits for them, and re-layouts: 8.03 us -> 19.7 us
    ppermute x24, starting transfers between devices: 29.6 us -> 18.7 us  [to_mode(): lax.ppermute(value, 'mode', [(m, (m + d) % modes) for m in range(modes)])]
  transfers between devices with their start and end apart: 80 -> 80, of which waited for: 22 -> 33; matrix products, arithmetic and copies ran while one was open for 9% -> 9% of each run, Pallas kernels for 14% -> 10%
where the time goes in v2:
time: 446 us; the launch traced here: 443 us
  waiting for transfers between devices  168 us (38%)
  starting transfers between devices  126 us (28%)
  Pallas kernels  84.1 us (19%)
  local copies, waits for them, and re-layouts  35.9 us (8%)
  other arithmetic  26.9 us (6%)
    ppermute x48, starting transfers between devices, to_along(): return lax.ppermute(value, 'chan', pairs)  97.6 us
    ppermute x48, waiting for transfers between devices, to_along(): return lax.ppermute(value, 'chan', pairs)  85.5 us
    ppermute x24, waiting for transfers between devices, to_mode(): lax.ppermute(value, 'mode', [(m, (m + d) % modes) for m in range(modes)])  71.9 us
    pallas_call x2, Pallas kernels, update(): pl.pallas_call(body, grid=(local_a,), in_specs=[spec] + [pl.BlockSpec((1,...  39.8 us
    pallas_call x2, Pallas kernels, narrow(): call(body, (local_a,), [pl.BlockSpec((ins, 1, 1, modes_b, out_ch), lambda...  21.1 us
    unnamed x135, local copies, waits for them, and re-layouts  19.7 us
    ppermute x24, starting transfers between devices, to_mode(): lax.ppermute(value, 'mode', [(m, (m + d) % modes) for m in range(modes)])  18.7 us
    pallas_call x4, Pallas kernels, gather_core(): call(body, (each,), [pl.BlockSpec((local_a, 1, ins, rank_out), lambda s:...  12.3 us
  transfers between devices with their start and end apart: 80, of which 33 were waited for; matrix products, arithmetic and copies ran while one was open for 9% of the time, Pallas kernels for 10%

profile of v2, /device:TPU:0, one launch (start us, length us, event | category | flops | bytes accessed | tf_op | source)
XLA Modules:
  0.0 443.2 jit_solution(17537901167390689386)
XLA Ops:
  4.1 11.0 %shard_map.103 = (f32[8,2,64,128]{3,2,1,0:T(8,128)S(1)}, f32[8,2,64,128]{3,2,1,0:T(8,128)S(1)}, f32[8,2,64,128]{3,2,1,0:T(8,128)}, f32[8,2,64,128]{3,2,1,0:T(8,1...) custom-call(bf16[64,2,8,32,256]{4,3,2,1,0:T(8,128)(2,1)} %grad_ref.3, ...), custom_call_target="tpu_custom_call" | custom-call | flops 4294967296 | bytes 12582912 | tf_op jit(solution)/shard_map/pallas_call | solution.py:80
  17.2 2.6 collective-permute-start.1
  21.4 1.6 multiply_bitcast_fusion
  23.1 2.5 copy.34
  25.6 2.8 reshape.80.refs_4_
  28.4 2.6 collective-permute-done.refs_1_
  31.0 1.7 collective-permute-done.1.refs_2_
  33.5 9.5 %collective-permute-done.2.refs_3_ = f32[8,2,64,128]{3,2,1,0:T(8,128)S(1)} collective-permute-done((f32[8,2,64,128]{3,2,1,0:T(8,128)}, f32[8,2,64,128]{3,2,1,0:T(8,128)S(1)}, u32[]{:S(2)}, u32[]{:S(2)}) %collective-permute-start.2) | collective-permute-done | bytes 524320 | tf_op jit(solution)/shard_map/ppermute | solution.py:240
  45.9 3.2 shard_map.104
  52.7 10.1 %shard_map.105 = (f32[8,2,64,128]{3,2,1,0:T(8,128)S(1)}, f32[8,2,64,128]{3,2,1,0:T(8,128)S(1)}, f32[8,2,64,128]{3,2,1,0:T(8,128)S(1)}, f32[8,2,64,128]{3,2,1,0:T...) custom-call(bf16[64,2,8,32,256]{4,3,2,1,0:T(8,128)(2,1)} %grad_ref.3, ...), custom_call_target="tpu_custom_call" | custom-call | flops 4294967296 | bytes 12582912 | tf_op jit(solution)/shard_map/pallas_call | solution.py:80
  67.9 6.5 %collective-permute-done.6.refs_3_ = f32[8,2,64,128]{3,2,1,0:T(8,128)} collective-permute-done((f32[8,2,64,128]{3,2,1,0:T(8,128)}, f32[8,2,64,128]{3,2,1,0:T(8,128)}, u32[]{:S(2)}, u32[]{:S(2)}) %collective-permute-start.6) | collective-permute-done | bytes 524320 | tf_op jit(solution)/shard_map/ppermute | solution.py:240
  75.1 1.8 add_bitcast_fusion.19
  76.9 4.5 %collective-permute-start.7 = (f32[16,2,16,128]{3,2,1,0:T(8,128)S(1)}, f32[16,2,16,128]{3,2,1,0:T(8,128)}, u32[]{:S(2)}, u32[]{:S(2)}) collective-permute-start(f32[16,2,16,128]{3,2,1,0:T(8,128)S(1)} %get-tuple-element.253), channel_id=1, source_target_pairs={{0,8},{4,12},{1,9},{5,13},{2,10},{6,14},{3,11},{7,15}} | collective-permute-start | bytes 786440 | tf_op jit(solution)/shard_map/ppermute | solution.py:254
  82.8 4.4 collective-permute-done.7
  87.2 1.8 bitcast_add_fusion.17
  89.0 5.2 %collective-permute-start.8 = (f32[16,2,16,128]{3,2,1,0:T(8,128)}, f32[16,2,16,128]{3,2,1,0:T(8,128)}, u32[]{:S(2)}, u32[]{:S(2)}) collective-permute-start(f32[16,2,16,128]{3,2,1,0:T(8,128)} %bitcast_add_fusion.17), channel_id=1, source_target_pairs={{0,8},{4,12},{8,16},{12,20},{1,9},{5,13},{9,17},{13,21},{2,10},{6,... | collective-permute-start | bytes 786440 | tf_op jit(solution)/shard_map/ppermute | solution.py:254
  95.2 4.1 shard_map.106
  100.1 2.2 bitcast_add_fusion.18
  103.7 4.3 collective-permute-start.9
  113.7 4.3 fusion.46
  118.0 5.6 %collective-permute-done.12 = f32[16,2,16,128]{3,2,1,0:T(8,128)S(1)} collective-permute-done((f32[16,2,16,128]{3,2,1,0:T(8,128)S(1)}, f32[16,2,16,128]{3,2,1,0:T(8,128)S(1)}, u32[]{:S(2)}, u32[]{:S(2)}) %collective-permute-start.12) | collective-permute-done | bytes 262176 | tf_op jit(solution)/shard_map/ppermute | solution.py:254
  124.7 6.9 %collective-permute-done.16.refs_3_ = f32[8,2,64,128]{3,2,1,0:T(8,128)S(1)} collective-permute-done((f32[8,2,64,128]{3,2,1,0:T(8,128)S(1)}, f32[8,2,64,128]{3,2,1,0:T(8,128)S(1)}, u32[]{:S(2)}, u32[]{:S(2)}) %collective-permute-start.16) | collective-permute-done | bytes 524320 | tf_op jit(solution)/shard_map/ppermute | solution.py:240
  132.8 4.0 collective-permute-start.23
  138.7 4.6 %collective-permute-start.18 = (f32[16,2,16,128]{3,2,1,0:T(8,128)S(1)}, f32[16,2,16,128]{3,2,1,0:T(8,128)S(1)}, u32[]{:S(2)}, u32[]{:S(2)}) collective-permute-start(f32[16,2,16,128]{3,2,1,0:T(8,128)S(1)} %fusion.31), channel_id=1, source_target_pairs={{0,8},{4,12},{8,16},{12,20},{16,24},{20,28},{1,9},{5,13},{9,17},{1... | collective-permute-start | bytes 786440 | tf_op jit(solution)/shard_map/ppermute | solution.py:254
  145.0 3.1 collective-permute-start.24
  151.0 4.2 collective-permute-done.24
  157.3 2.5 shard_map.107
  160.6 5.0 %collective-permute-start.25 = (f32[16,2,16,128]{3,2,1,0:T(8,128)S(1)}, f32[16,2,16,128]{3,2,1,0:T(8,128)S(1)}, u32[]{:S(2)}, u32[]{:S(2)}) collective-permute-start(f32[16,2,16,128]{3,2,1,0:T(8,128)S(1)} %get-tuple-element.247), channel_id=1, source_target_pairs={{0,8},{4,12},{8,16},{12,20},{16,24},{20,28},{1,9},{5,13},{9,17},{1... | collective-permute-start | bytes 786440 | tf_op jit(solution)/shard_map/ppermute | solution.py:254
  168.7 6.5 %collective-permute-done.22 = f32[16,2,16,128]{3,2,1,0:T(8,128)S(1)} collective-permute-done((f32[16,2,16,128]{3,2,1,0:T(8,128)S(1)}, f32[16,2,16,128]{3,2,1,0:T(8,128)S(1)}, u32[]{:S(2)}, u32[]{:S(2)}) %collective-permute-start.22) | collective-permute-done | bytes 262176 | tf_op jit(solution)/shard_map/ppermute | solution.py:254
  177.5 9.1 %collective-permute-done.28 = f32[16,2,16,128]{3,2,1,0:T(8,128)S(1)} collective-permute-done((f32[16,2,16,128]{3,2,1,0:T(8,128)S(1)}, f32[16,2,16,128]{3,2,1,0:T(8,128)S(1)}, u32[]{:S(2)}, u32[]{:S(2)}) %collective-permute-start.28) | collective-permute-done | bytes 262176 | tf_op jit(solution)/shard_map/ppermute | solution.py:254
  187.7 3.6 collective-permute-done.32.refs_3_
  194.8 4.6 %collective-permute-start.35 = (f32[16,2,16,128]{3,2,1,0:T(8,128)S(1)}, f32[16,2,16,128]{3,2,1,0:T(8,128)S(1)}, u32[]{:S(2)}, u32[]{:S(2)}) collective-permute-start(f32[16,2,16,128]{3,2,1,0:T(8,128)S(1)} %fusion.33), channel_id=1, source_target_pairs={{0,8},{4,12},{8,16},{12,20},{16,24},{20,28},{1,9},{5,13},{9,17},{1... | collective-permute-start | bytes 786440 | tf_op jit(solution)/shard_map/ppermute | solution.py:254
  200.1 3.0 collective-permute-start.41
  206.7 4.7 %collective-permute-done.41 = f32[16,2,16,128]{3,2,1,0:T(8,128)S(1)} collective-permute-done((f32[16,2,16,128]{3,2,1,0:T(8,128)S(1)}, f32[16,2,16,128]{3,2,1,0:T(8,128)S(1)}, u32[]{:S(2)}, u32[]{:S(2)}) %collective-permute-start.41) | collective-permute-done | bytes 262176 | tf_op jit(solution)/shard_map/ppermute | solution.py:254
  212.2 2.5 shard_map.108
  214.7 1.7 collective-permute-start.46
  216.4 5.0 %collective-permute-start.42 = (f32[16,2,16,128]{3,2,1,0:T(8,128)S(1)}, f32[16,2,16,128]{3,2,1,0:T(8,128)S(1)}, u32[]{:S(2)}, u32[]{:S(2)}) collective-permute-start(f32[16,2,16,128]{3,2,1,0:T(8,128)S(1)} %get-tuple-element.243), channel_id=1, source_target_pairs={{0,8},{4,12},{8,16},{12,20},{16,24},{20,28},{1,9},{5,13},{9,17},{1... | collective-permute-start | bytes 786440 | tf_op jit(solution)/shard_map/ppermute | solution.py:254
  223.6 8.1 %collective-permute-done.39 = f32[16,2,16,128]{3,2,1,0:T(8,128)S(1)} collective-permute-done((f32[16,2,16,128]{3,2,1,0:T(8,128)S(1)}, f32[16,2,16,128]{3,2,1,0:T(8,128)S(1)}, u32[]{:S(2)}, u32[]{:S(2)}) %collective-permute-start.39) | collective-permute-done | bytes 262176 | tf_op jit(solution)/shard_map/ppermute | solution.py:254
  233.2 7.9 %collective-permute-done.45 = f32[16,2,16,128]{3,2,1,0:T(8,128)S(1)} collective-permute-done((f32[16,2,16,128]{3,2,1,0:T(8,128)S(1)}, f32[16,2,16,128]{3,2,1,0:T(8,128)S(1)}, u32[]{:S(2)}, u32[]{:S(2)}) %collective-permute-start.45) | collective-permute-done | bytes 262176 | tf_op jit(solution)/shard_map/ppermute | solution.py:254
  241.2 10.3 %collective-permute-done.46 = f32[4,16,2,16,128]{4,3,2,1,0:T(8,128)S(1)} collective-permute-done((f32[4,16,2,16,128]{4,3,2,1,0:T(8,128)S(1)}, f32[4,16,2,16,128]{4,3,2,1,0:T(8,128)S(1)}, u32[]{:S(2)}, u32[]{:S(2)}) %collective-permute-start.46) | collective-permute-done | bytes 1048608 | tf_op jit(solution)/shard_map/ppermute | solution.py:248
  252.4 1.9 collective-permute-start.57
  258.3 5.3 %collective-permute-start.52 = (f32[16,2,16,128]{3,2,1,0:T(8,128)}, f32[16,2,16,128]{3,2,1,0:T(8,128)}, u32[]{:S(2)}, u32[]{:S(2)}) collective-permute-start(f32[16,2,16,128]{3,2,1,0:T(8,128)} %fusion.35), channel_id=1, source_target_pairs={{0,8},{4,12},{8,16},{12,20},{16,24},{20,28},{1,9},{5,13},{9,17},{1... | collective-permute-start | bytes 786440 | tf_op jit(solution)/shard_map/ppermute | solution.py:254
  265.7 2.0 collective-permute-start.58
  267.8 2.7 reshape.83.refs_2_
  276.1 2.5 shard_map.109
  280.3 4.8 %collective-permute-start.59 = (f32[16,2,16,128]{3,2,1,0:T(8,128)S(1)}, f32[16,2,16,128]{3,2,1,0:T(8,128)S(1)}, u32[]{:S(2)}, u32[]{:S(2)}) collective-permute-start(f32[16,2,16,128]{3,2,1,0:T(8,128)S(1)} %get-tuple-element.239), channel_id=1, source_target_pairs={{0,8},{4,12},{8,16},{12,20},{16,24},{20,28},{1,9},{5,13},{9,17},{1... | collective-permute-start | bytes 786440 | tf_op jit(solution)/shard_map/ppermute | solution.py:254
  287.2 8.9 %collective-permute-done.56 = f32[16,2,16,128]{3,2,1,0:T(8,128)S(1)} collective-permute-done((f32[16,2,16,128]{3,2,1,0:T(8,128)S(1)}, f32[16,2,16,128]{3,2,1,0:T(8,128)S(1)}, u32[]{:S(2)}, u32[]{:S(2)}) %collective-permute-start.56) | collective-permute-done | bytes 262176 | tf_op jit(solution)/shard_map/ppermute | solution.py:254
  301.1 7.6 %collective-permute-done.62 = f32[16,2,16,128]{3,2,1,0:T(8,128)S(1)} collective-permute-done((f32[16,2,16,128]{3,2,1,0:T(8,128)S(1)}, f32[16,2,16,128]{3,2,1,0:T(8,128)S(1)}, u32[]{:S(2)}, u32[]{:S(2)}) %collective-permute-start.62) | collective-permute-done | bytes 262176 | tf_op jit(solution)/shard_map/ppermute | solution.py:254
  310.1 3.6 collective-permute-done.49.refs_6_
  315.6 4.6 %collective-permute-start.68 = (f32[16,2,16,128]{3,2,1,0:T(8,128)S(1)}, f32[16,2,16,128]{3,2,1,0:T(8,128)S(1)}, u32[]{:S(2)}, u32[]{:S(2)}) collective-permute-start(f32[16,2,16,128]{3,2,1,0:T(8,128)S(1)} %fusion.37), channel_id=1, source_target_pairs={{0,8},{4,12},{8,16},{12,20},{16,24},{20,28},{1,9},{5,13},{9,17},{1... | collective-permute-start | bytes 786440 | tf_op jit(solution)/shard_map/ppermute | solution.py:254
  320.2 4.3 collective-permute-done.67
  328.3 6.9 %collective-permute-done.71 = f32[16,2,16,128]{3,2,1,0:T(8,128)S(1)} collective-permute-done((f32[16,2,16,128]{3,2,1,0:T(8,128)S(1)}, f32[16,2,16,128]{3,2,1,0:T(8,128)S(1)}, u32[]{:S(2)}, u32[]{:S(2)}) %collective-permute-start.71) | collective-permute-done | bytes 262176 | tf_op jit(solution)/shard_map/ppermute | solution.py:254
  336.6 2.5 shard_map.110
  341.4 3.9 collective-permute-done.72
  345.4 7.4 %collective-permute-done.63.refs_3_ = f32[8,2,64,128]{3,2,1,0:T(8,128)S(1)} collective-permute-done((f32[8,2,64,128]{3,2,1,0:T(8,128)S(1)}, f32[8,2,64,128]{3,2,1,0:T(8,128)S(1)}, u32[]{:S(2)}, u32[]{:S(2)}) %collective-permute-start.63) | collective-permute-done | bytes 524320 | tf_op jit(solution)/shard_map/ppermute | solution.py:240
  354.8 8.8 %collective-permute-done.65.refs_7_ = f32[8,2,64,128]{3,2,1,0:T(8,128)S(1)} collective-permute-done((f32[8,2,64,128]{3,2,1,0:T(8,128)S(1)}, f32[8,2,64,128]{3,2,1,0:T(8,128)S(1)}, u32[]{:S(2)}, u32[]{:S(2)}) %collective-permute-start.65) | collective-permute-done | bytes 524320 | tf_op jit(solution)/shard_map/ppermute | solution.py:240
  365.4 1.9 reshape.85
  368.3 2.5 shard_map.111
  375.5 7.7 %collective-permute-done.73.refs_2_ = f32[8,2,64,128]{3,2,1,0:T(8,128)S(1)} collective-permute-done((f32[8,2,64,128]{3,2,1,0:T(8,128)S(1)}, f32[8,2,64,128]{3,2,1,0:T(8,128)S(1)}, u32[]{:S(2)}, u32[]{:S(2)}) %collective-permute-start.73) | collective-permute-done | bytes 524320 | tf_op jit(solution)/shard_map/ppermute | solution.py:240
  383.2 4.0 collective-permute-done.74.refs_4_
  387.2 8.0 %collective-permute-done.75.refs_6_ = f32[8,2,64,128]{3,2,1,0:T(8,128)S(1)} collective-permute-done((f32[8,2,64,128]{3,2,1,0:T(8,128)S(1)}, f32[8,2,64,128]{3,2,1,0:T(8,128)S(1)}, u32[]{:S(2)}, u32[]{:S(2)}) %collective-permute-start.75) | collective-permute-done | bytes 524320 | tf_op jit(solution)/shard_map/ppermute | solution.py:240
  395.2 3.5 shard_map.112
  403.4 19.9 %shard_map.113.refs_10_ = bf16[64,2,8,32,256]{4,3,2,1,0:T(8,128)(2,1)} custom-call(bf16[64,2,8,32,256]{4,3,2,1,0:T(8,128)(2,1)} %weight_ref.3, f32[8,2,64,128]{3,2,1,0:T(8,128)S(1)} %copy-done.6, f32[8,2,64,128]{3,2,1,0:T(8,128)S(1)} %copy-done.14, f32[8,2,64,128]{3,2,1,0:T(8,128)S(1)} %copy-done.8, f32[8,2,64,128]{3,2,1,0:T(8,128)S(1)} %copy-done.16, ...), custom_call_target="tpu_custom_call" | custom-call | flops 4294967296 | bytes 20971520 | tf_op jit(solution)/shard_map/pallas_call | solution.py:191
  423.3 19.9 %shard_map.114 = bf16[64,2,8,32,256]{4,3,2,1,0:T(8,128)(2,1)} custom-call(bf16[64,2,8,32,256]{4,3,2,1,0:T(8,128)(2,1)} %weight_ref.3, f32[8,2,64,128]{3,2,1,0:T(8,128)S(1)} %get-tuple-element.199.refs_0_, f32[8,2,64,128]{3,2,1,0:T(8,128)S(1)} %get-tuple-element.206.refs_1_, ...), custom_call_target="tpu_custom_call", output_to_operand_aliasing={{}: (11, {})} | custom-call | flops 4294967296 | bytes 20971520 | tf_op jit(solution)/shard_map/pallas_call | solution.py:191
  (314 shorter events, 106.7 us)
Async XLA Ops:
  16.7 14.3 %collective-permute-start = (f32[8,2,64,128]{3,2,1,0:T(8,128)}, f32[8,2,64,128]{3,2,1,0:T(8,128)S(1)}, u32[]{:S(2)}, u32[]{:S(2)}) collective-permute-start(f32[8,2,64,128]{3,2,1,0:T(8,128)} %get-tuple-element.113), channel_id=1, source_target_pairs={{0,1},{1,2},{2,3},{3,0},{4,5},{5,6},{6,7},{7,4},{8,9},{9,10},{10,1... | collective-permute-start | bytes 1572872 | tf_op jit(solution)/shard_map/ppermute | solution.py:240
  17.2 15.5 %collective-permute-start.1 = (f32[8,2,64,128]{3,2,1,0:T(8,128)}, f32[8,2,64,128]{3,2,1,0:T(8,128)S(1)}, u32[]{:S(2)}, u32[]{:S(2)}) collective-permute-start(f32[8,2,64,128]{3,2,1,0:T(8,128)} %get-tuple-element.114), channel_id=1, source_target_pairs={{0,2},{1,3},{2,0},{3,1},{4,6},{5,7},{6,4},{7,5},{8,10},{9,11},{10,... | collective-permute-start | bytes 1572872 | tf_op jit(solution)/shard_map/ppermute | solution.py:240
  19.7 23.3 %collective-permute-start.2 = (f32[8,2,64,128]{3,2,1,0:T(8,128)}, f32[8,2,64,128]{3,2,1,0:T(8,128)S(1)}, u32[]{:S(2)}, u32[]{:S(2)}) collective-permute-start(f32[8,2,64,128]{3,2,1,0:T(8,128)} %get-tuple-element.115), channel_id=1, source_target_pairs={{0,3},{1,0},{2,1},{3,2},{4,7},{5,4},{6,5},{7,6},{8,11},{9,8},{10,9... | collective-permute-start | bytes 1572872 | tf_op jit(solution)/shard_map/ppermute | solution.py:240
  49.0 26.0 %collective-permute-start.3 = (f32[4,16,2,16,128]{4,3,2,1,0:T(8,128)}, f32[4,16,2,16,128]{4,3,2,1,0:T(8,128)}, u32[]{:S(2)}, u32[]{:S(2)}) collective-permute-start(f32[4,16,2,16,128]{4,3,2,1,0:T(8,128)} %get-tuple-element.125), channel_id=1, source_target_pairs={{0,4},{4,0},{8,12},{12,8},{16,20},{20,16},{24,28},{28,24},{1,5},{5... | collective-permute-start | bytes 3145736 | tf_op jit(solution)/shard_map/ppermute | solution.py:248
  50.5 16.4 %collective-permute-start.4 = (f32[8,2,64,128]{3,2,1,0:T(8,128)}, f32[8,2,64,128]{3,2,1,0:T(8,128)S(1)}, u32[]{:S(2)}, u32[]{:S(2)}) collective-permute-start(f32[8,2,64,128]{3,2,1,0:T(8,128)} %copy-done.41), channel_id=1, source_target_pairs={{0,1},{1,2},{2,3},{3,0},{4,5},{5,6},{6,7},{7,4},{8,9},{9,10},{10,1... | collective-permute-start | bytes 1572872 | tf_op jit(solution)/shard_map/ppermute | solution.py:240
  51.2 16.5 %collective-permute-start.5 = (f32[8,2,64,128]{3,2,1,0:T(8,128)}, f32[8,2,64,128]{3,2,1,0:T(8,128)}, u32[]{:S(2)}, u32[]{:S(2)}) collective-permute-start(f32[8,2,64,128]{3,2,1,0:T(8,128)} %copy-done.40), channel_id=1, source_target_pairs={{0,2},{1,3},{2,0},{3,1},{4,6},{5,7},{6,4},{7,5},{8,10},{9,11},{10,... | collective-permute-start | bytes 1572872 | tf_op jit(solution)/shard_map/ppermute | solution.py:240
  52.7 21.7 %collective-permute-start.6 = (f32[8,2,64,128]{3,2,1,0:T(8,128)}, f32[8,2,64,128]{3,2,1,0:T(8,128)}, u32[]{:S(2)}, u32[]{:S(2)}) collective-permute-start(f32[8,2,64,128]{3,2,1,0:T(8,128)} %copy-done.38), channel_id=1, source_target_pairs={{0,3},{1,0},{2,1},{3,2},{4,7},{5,4},{6,5},{7,6},{8,11},{9,8},{10,9... | collective-permute-start | bytes 1572872 | tf_op jit(solution)/shard_map/ppermute | solution.py:240
  76.9 10.3 %collective-permute-start.7 = (f32[16,2,16,128]{3,2,1,0:T(8,128)S(1)}, f32[16,2,16,128]{3,2,1,0:T(8,128)}, u32[]{:S(2)}, u32[]{:S(2)}) collective-permute-start(f32[16,2,16,128]{3,2,1,0:T(8,128)S(1)} %get-tuple-element.253), channel_id=1, source_target_pairs={{0,8},{4,12},{1,9},{5,13},{2,10},{6,14},{3,11},{7,15}} | collective-permute-start | bytes 786440 | tf_op jit(solution)/shard_map/ppermute | solution.py:254
  81.4 18.8 %collective-permute-start.10 = (f32[16,2,16,128]{3,2,1,0:T(8,128)}, f32[16,2,16,128]{3,2,1,0:T(8,128)}, u32[]{:S(2)}, u32[]{:S(2)}) collective-permute-start(f32[16,2,16,128]{3,2,1,0:T(8,128)} %get-tuple-element.254), channel_id=1, source_target_pairs={{24,16},{28,20},{25,17},{29,21},{26,18},{30,22},{27,19},{31,23}} | collective-permute-start | bytes 786440 | tf_op jit(solution)/shard_map/ppermute | solution.py:254
  89.0 11.2 %collective-permute-start.8 = (f32[16,2,16,128]{3,2,1,0:T(8,128)}, f32[16,2,16,128]{3,2,1,0:T(8,128)}, u32[]{:S(2)}, u32[]{:S(2)}) collective-permute-start(f32[16,2,16,128]{3,2,1,0:T(8,128)} %bitcast_add_fusion.17), channel_id=1, source_target_pairs={{0,8},{4,12},{8,16},{12,20},{1,9},{5,13},{9,17},{13,21},{2,10},{6,... | collective-permute-start | bytes 786440 | tf_op jit(solution)/shard_map/ppermute | solution.py:254
  99.3 32.3 %collective-permute-start.13 = (f32[4,16,2,16,128]{4,3,2,1,0:T(8,128)}, f32[4,16,2,16,128]{4,3,2,1,0:T(8,128)}, u32[]{:S(2)}, u32[]{:S(2)}) collective-permute-start(f32[4,16,2,16,128]{4,3,2,1,0:T(8,128)} %get-tuple-element.142), channel_id=1, source_target_pairs={{0,4},{4,0},{8,12},{12,8},{16,20},{20,16},{24,28},{28,24},{1,5},{5... | collective-permute-start | bytes 3145736 | tf_op jit(solution)/shard_map/ppermute | solution.py:248
  108.0 16.7 %collective-permute-start.14 = (f32[8,2,64,128]{3,2,1,0:T(8,128)}, f32[8,2,64,128]{3,2,1,0:T(8,128)S(1)}, u32[]{:S(2)}, u32[]{:S(2)}) collective-permute-start(f32[8,2,64,128]{3,2,1,0:T(8,128)} %copy-done.39), channel_id=1, source_target_pairs={{0,1},{1,2},{2,3},{3,0},{4,5},{5,6},{6,7},{7,4},{8,9},{9,10},{10,1... | collective-permute-start | bytes 1572872 | tf_op jit(solution)/shard_map/ppermute | solution.py:240
  108.0 16.7 %collective-permute-start.15 = (f32[8,2,64,128]{3,2,1,0:T(8,128)}, f32[8,2,64,128]{3,2,1,0:T(8,128)S(1)}, u32[]{:S(2)}, u32[]{:S(2)}) collective-permute-start(f32[8,2,64,128]{3,2,1,0:T(8,128)} %copy-done.37), channel_id=1, source_target_pairs={{0,2},{1,3},{2,0},{3,1},{4,6},{5,7},{6,4},{7,5},{8,10},{9,11},{10,... | collective-permute-start | bytes 1572872 | tf_op jit(solution)/shard_map/ppermute | solution.py:240
  108.5 23.1 %collective-permute-start.16 = (f32[8,2,64,128]{3,2,1,0:T(8,128)S(1)}, f32[8,2,64,128]{3,2,1,0:T(8,128)S(1)}, u32[]{:S(2)}, u32[]{:S(2)}) collective-permute-start(f32[8,2,64,128]{3,2,1,0:T(8,128)S(1)} %copy-done.36), channel_id=1, source_target_pairs={{0,3},{1,0},{2,1},{3,2},{4,7},{5,4},{6,5},{7,6},{8,11},{9,8},{10,9... | collective-permute-start | bytes 1572872 | tf_op jit(solution)/shard_map/ppermute | solution.py:240
  112.4 11.2 %collective-permute-start.12 = (f32[16,2,16,128]{3,2,1,0:T(8,128)S(1)}, f32[16,2,16,128]{3,2,1,0:T(8,128)S(1)}, u32[]{:S(2)}, u32[]{:S(2)}) collective-permute-start(f32[16,2,16,128]{3,2,1,0:T(8,128)S(1)} %bitcast_add_fusion.16), channel_id=1, source_target_pairs={{8,0},{12,4},{16,8},{20,12},{24,16},{28,20},{9,1},{13,5},{17,9},{2... | collective-permute-start | bytes 786440 | tf_op jit(solution)/shard_map/ppermute | solution.py:254
  132.8 11.2 %collective-permute-start.23 = (f32[16,2,16,128]{3,2,1,0:T(8,128)S(1)}, f32[16,2,16,128]{3,2,1,0:T(8,128)S(1)}, u32[]{:S(2)}, u32[]{:S(2)}) collective-permute-start(f32[16,2,16,128]{3,2,1,0:T(8,128)S(1)} %get-tuple-element.249), channel_id=1, source_target_pairs={{0,8},{4,12},{1,9},{5,13},{2,10},{6,14},{3,11},{7,15}} | collective-permute-start | bytes 786440 | tf_op jit(solution)/shard_map/ppermute | solution.py:254
  137.4 11.4 %collective-permute-start.17 = (f32[16,2,16,128]{3,2,1,0:T(8,128)S(1)}, f32[16,2,16,128]{3,2,1,0:T(8,128)S(1)}, u32[]{:S(2)}, u32[]{:S(2)}) collective-permute-start(f32[16,2,16,128]{3,2,1,0:T(8,128)S(1)} %fusion.31), channel_id=1, source_target_pairs={{8,0},{12,4},{16,8},{20,12},{24,16},{28,20},{9,1},{13,5},{17,9},{2... | collective-permute-start | bytes 786440 | tf_op jit(solution)/shard_map/ppermute | solution.py:254
  138.7 11.6 %collective-permute-start.18 = (f32[16,2,16,128]{3,2,1,0:T(8,128)S(1)}, f32[16,2,16,128]{3,2,1,0:T(8,128)S(1)}, u32[]{:S(2)}, u32[]{:S(2)}) collective-permute-start(f32[16,2,16,128]{3,2,1,0:T(8,128)S(1)} %fusion.31), channel_id=1, source_target_pairs={{0,8},{4,12},{8,16},{12,20},{16,24},{20,28},{1,9},{5,13},{9,17},{1... | collective-permute-start | bytes 786440 | tf_op jit(solution)/shard_map/ppermute | solution.py:254
  145.0 10.3 %collective-permute-start.24 = (f32[16,2,16,128]{3,2,1,0:T(8,128)S(1)}, f32[16,2,16,128]{3,2,1,0:T(8,128)S(1)}, u32[]{:S(2)}, u32[]{:S(2)}) collective-permute-start(f32[16,2,16,128]{3,2,1,0:T(8,128)S(1)} %bitcast_add_fusion.12), channel_id=1, source_target_pairs={{0,8},{4,12},{8,16},{12,20},{1,9},{5,13},{9,17},{13,21},{2,10},{6,... | collective-permute-start | bytes 786440 | tf_op jit(solution)/shard_map/ppermute | solution.py:254
  148.1 39.6 %collective-permute-start.30 = (f32[8,2,64,128]{3,2,1,0:T(8,128)S(1)}, f32[8,2,64,128]{3,2,1,0:T(8,128)S(1)}, u32[]{:S(2)}, u32[]{:S(2)}) collective-permute-start(f32[8,2,64,128]{3,2,1,0:T(8,128)S(1)} %copy-done.34), channel_id=1, source_target_pairs={{0,1},{1,2},{2,3},{3,0},{4,5},{5,6},{6,7},{7,4},{8,9},{9,10},{10,1... | collective-permute-start | bytes 1572872 | tf_op jit(solution)/shard_map/ppermute | solution.py:240
  148.8 11.8 %collective-permute-start.21 = (f32[16,2,16,128]{3,2,1,0:T(8,128)S(1)}, f32[16,2,16,128]{3,2,1,0:T(8,128)S(1)}, u32[]{:S(2)}, u32[]{:S(2)}) collective-permute-start(f32[16,2,16,128]{3,2,1,0:T(8,128)S(1)} %collective-permute-done.17), channel_id=1, source_target_pairs={{8,0},{12,4},{16,8},{20,12},{9,1},{13,5},{17,9},{21,13},{10,2},{14... | collective-permute-start | bytes 786440 | tf_op jit(solution)/shard_map/ppermute | solution.py:254
  150.3 15.3 %collective-permute-start.19 = (f32[16,2,16,128]{3,2,1,0:T(8,128)S(1)}, f32[16,2,16,128]{3,2,1,0:T(8,128)S(1)}, u32[]{:S(2)}, u32[]{:S(2)}) collective-permute-start(f32[16,2,16,128]{3,2,1,0:T(8,128)S(1)} %collective-permute-done.18), channel_id=1, source_target_pairs={{8,16},{12,20},{16,24},{20,28},{9,17},{13,21},{17,25},{21,29},{10,... | collective-permute-start | bytes 786440 | tf_op jit(solution)/shard_map/ppermute | solution.py:254
  156.5 10.5 %collective-permute-start.27 = (f32[16,2,16,128]{3,2,1,0:T(8,128)S(1)}, f32[16,2,16,128]{3,2,1,0:T(8,128)S(1)}, u32[]{:S(2)}, u32[]{:S(2)}) collective-permute-start(f32[16,2,16,128]{3,2,1,0:T(8,128)S(1)} %get-tuple-element.248), channel_id=1, source_target_pairs={{16,8},{20,12},{24,16},{28,20},{17,9},{21,13},{25,17},{29,21},{18,... | collective-permute-start | bytes 786440 | tf_op jit(solution)/shard_map/ppermute | solution.py:254
  159.8 31.5 %collective-permute-start.29 = (f32[4,16,2,16,128]{4,3,2,1,0:T(8,128)S(1)}, f32[4,16,2,16,128]{4,3,2,1,0:T(8,128)S(1)}, u32[]{:S(2)}, u32[]{:S(2)}) collective-permute-start(f32[4,16,2,16,128]{4,3,2,1,0:T(8,128)S(1)} %get-tuple-element.159), channel_id=1, source_target_pairs={{0,4},{4,0},{8,12},{12,8},{16,20},{20,16},{24,28},{28,24},{1,5},{5... | collective-permute-start | bytes 3145736 | tf_op jit(solution)/shard_map/ppermute | solution.py:248
  160.6 15.5 %collective-permute-start.25 = (f32[16,2,16,128]{3,2,1,0:T(8,128)S(1)}, f32[16,2,16,128]{3,2,1,0:T(8,128)S(1)}, u32[]{:S(2)}, u32[]{:S(2)}) collective-permute-start(f32[16,2,16,128]{3,2,1,0:T(8,128)S(1)} %get-tuple-element.247), channel_id=1, source_target_pairs={{0,8},{4,12},{8,16},{12,20},{16,24},{20,28},{1,9},{5,13},{9,17},{1... | collective-permute-start | bytes 786440 | tf_op jit(solution)/shard_map/ppermute | solution.py:254
  175.2 12.5 %collective-permute-start.31 = (f32[8,2,64,128]{3,2,1,0:T(8,128)S(1)}, f32[8,2,64,128]{3,2,1,0:T(8,128)S(1)}, u32[]{:S(2)}, u32[]{:S(2)}) collective-permute-start(f32[8,2,64,128]{3,2,1,0:T(8,128)S(1)} %copy-done.32), channel_id=1, source_target_pairs={{0,2},{1,3},{2,0},{3,1},{4,6},{5,7},{6,4},{7,5},{8,10},{9,11},{10,... | collective-permute-start | bytes 1572872 | tf_op jit(solution)/shard_map/ppermute | solution.py:240
  176.0 15.3 %collective-permute-start.32 = (f32[8,2,64,128]{3,2,1,0:T(8,128)S(1)}, f32[8,2,64,128]{3,2,1,0:T(8,128)S(1)}, u32[]{:S(2)}, u32[]{:S(2)}) collective-permute-start(f32[8,2,64,128]{3,2,1,0:T(8,128)S(1)} %copy-done.30), channel_id=1, source_target_pairs={{0,3},{1,0},{2,1},{3,2},{4,7},{5,4},{6,5},{7,6},{8,11},{9,8},{10,9... | collective-permute-start | bytes 1572872 | tf_op jit(solution)/shard_map/ppermute | solution.py:240
  176.1 10.6 %collective-permute-start.28 = (f32[16,2,16,128]{3,2,1,0:T(8,128)S(1)}, f32[16,2,16,128]{3,2,1,0:T(8,128)S(1)}, u32[]{:S(2)}, u32[]{:S(2)}) collective-permute-start(f32[16,2,16,128]{3,2,1,0:T(8,128)S(1)} %bitcast_add_fusion.11), channel_id=1, source_target_pairs={{8,0},{12,4},{16,8},{20,12},{24,16},{28,20},{9,1},{13,5},{17,9},{2... | collective-permute-start | bytes 786440 | tf_op jit(solution)/shard_map/ppermute | solution.py:254
  193.4 11.3 %collective-permute-start.34 = (f32[16,2,16,128]{3,2,1,0:T(8,128)S(1)}, f32[16,2,16,128]{3,2,1,0:T(8,128)S(1)}, u32[]{:S(2)}, u32[]{:S(2)}) collective-permute-start(f32[16,2,16,128]{3,2,1,0:T(8,128)S(1)} %fusion.33), channel_id=1, source_target_pairs={{8,0},{12,4},{16,8},{20,12},{24,16},{28,20},{9,1},{13,5},{17,9},{2... | collective-permute-start | bytes 786440 | tf_op jit(solution)/shard_map/ppermute | solution.py:254
  194.8 11.2 %collective-permute-start.35 = (f32[16,2,16,128]{3,2,1,0:T(8,128)S(1)}, f32[16,2,16,128]{3,2,1,0:T(8,128)S(1)}, u32[]{:S(2)}, u32[]{:S(2)}) collective-permute-start(f32[16,2,16,128]{3,2,1,0:T(8,128)S(1)} %fusion.33), channel_id=1, source_target_pairs={{0,8},{4,12},{8,16},{12,20},{16,24},{20,28},{1,9},{5,13},{9,17},{1... | collective-permute-start | bytes 786440 | tf_op jit(solution)/shard_map/ppermute | solution.py:254
  200.1 11.2 %collective-permute-start.41 = (f32[16,2,16,128]{3,2,1,0:T(8,128)S(1)}, f32[16,2,16,128]{3,2,1,0:T(8,128)S(1)}, u32[]{:S(2)}, u32[]{:S(2)}) collective-permute-start(f32[16,2,16,128]{3,2,1,0:T(8,128)S(1)} %bitcast_add_fusion.7), channel_id=1, source_target_pairs={{0,8},{4,12},{8,16},{12,20},{1,9},{5,13},{9,17},{13,21},{2,10},{6,... | collective-permute-start | bytes 786440 | tf_op jit(solution)/shard_map/ppermute | solution.py:254
  203.1 38.1 %collective-permute-start.33 = (f32[4,16,2,16,128]{4,3,2,1,0:T(8,128)S(1)}, f32[4,16,2,16,128]{4,3,2,1,0:T(8,128)S(1)}, u32[]{:S(2)}, u32[]{:S(2)}) collective-permute-start(f32[4,16,2,16,128]{4,3,2,1,0:T(8,128)S(1)} %pad_maximum_fusion.refs_0_), channel_id=1, source_target_pairs={{0,4},{4,0},{8,12},{12,8},{16,20},{20,16},{24,28},{28,24},{1,5},{5... | collective-permute-start | bytes 3145736 | tf_op jit(solution)/shard_map/ppermute | solution.py:248
  204.7 11.7 %collective-permute-start.38 = (f32[16,2,16,128]{3,2,1,0:T(8,128)S(1)}, f32[16,2,16,128]{3,2,1,0:T(8,128)S(1)}, u32[]{:S(2)}, u32[]{:S(2)}) collective-permute-start(f32[16,2,16,128]{3,2,1,0:T(8,128)S(1)} %collective-permute-done.34), channel_id=1, source_target_pairs={{8,0},{12,4},{16,8},{20,12},{9,1},{13,5},{17,9},{21,13},{10,2},{14... | collective-permute-start | bytes 786440 | tf_op jit(solution)/shard_map/ppermute | solution.py:254
  206.0 15.5 %collective-permute-start.36 = (f32[16,2,16,128]{3,2,1,0:T(8,128)S(1)}, f32[16,2,16,128]{3,2,1,0:T(8,128)S(1)}, u32[]{:S(2)}, u32[]{:S(2)}) collective-permute-start(f32[16,2,16,128]{3,2,1,0:T(8,128)S(1)} %collective-permute-done.35), channel_id=1, source_target_pairs={{8,16},{12,20},{16,24},{20,28},{9,17},{13,21},{17,25},{21,29},{10,... | collective-permute-start | bytes 786440 | tf_op jit(solution)/shard_map/ppermute | solution.py:254
  211.5 11.3 %collective-permute-start.44 = (f32[16,2,16,128]{3,2,1,0:T(8,128)S(1)}, f32[16,2,16,128]{3,2,1,0:T(8,128)S(1)}, u32[]{:S(2)}, u32[]{:S(2)}) collective-permute-start(f32[16,2,16,128]{3,2,1,0:T(8,128)S(1)} %get-tuple-element.244), channel_id=1, source_target_pairs={{16,8},{20,12},{24,16},{28,20},{17,9},{21,13},{25,17},{29,21},{18,... | collective-permute-start | bytes 786440 | tf_op jit(solution)/shard_map/ppermute | solution.py:254
  214.7 36.8 %collective-permute-start.46 = (f32[4,16,2,16,128]{4,3,2,1,0:T(8,128)S(1)}, f32[4,16,2,16,128]{4,3,2,1,0:T(8,128)S(1)}, u32[]{:S(2)}, u32[]{:S(2)}) collective-permute-start(f32[4,16,2,16,128]{4,3,2,1,0:T(8,128)S(1)} %get-tuple-element.173), channel_id=1, source_target_pairs={{0,4},{4,0},{8,12},{12,8},{16,20},{20,16},{24,28},{28,24},{1,5},{5... | collective-permute-start | bytes 3145736 | tf_op jit(solution)/shard_map/ppermute | solution.py:248
  216.4 16.7 %collective-permute-start.42 = (f32[16,2,16,128]{3,2,1,0:T(8,128)S(1)}, f32[16,2,16,128]{3,2,1,0:T(8,128)S(1)}, u32[]{:S(2)}, u32[]{:S(2)}) collective-permute-start(f32[16,2,16,128]{3,2,1,0:T(8,128)S(1)} %get-tuple-element.243), channel_id=1, source_target_pairs={{0,8},{4,12},{8,16},{12,20},{16,24},{20,28},{1,9},{5,13},{9,17},{1... | collective-permute-start | bytes 786440 | tf_op jit(solution)/shard_map/ppermute | solution.py:254
  221.5 10.2 %collective-permute-start.39 = (f32[16,2,16,128]{3,2,1,0:T(8,128)S(1)}, f32[16,2,16,128]{3,2,1,0:T(8,128)S(1)}, u32[]{:S(2)}, u32[]{:S(2)}) collective-permute-start(f32[16,2,16,128]{3,2,1,0:T(8,128)S(1)} %collective-permute-done.38), channel_id=1, source_target_pairs={{8,0},{12,4},{9,1},{13,5},{10,2},{14,6},{11,3},{15,7}} | collective-permute-start | bytes 786440 | tf_op jit(solution)/shard_map/ppermute | solution.py:254
  252.4 12.5 %collective-permute-start.57 = (f32[16,2,16,128]{3,2,1,0:T(8,128)S(1)}, f32[16,2,16,128]{3,2,1,0:T(8,128)S(1)}, u32[]{:S(2)}, u32[]{:S(2)}) collective-permute-start(f32[16,2,16,128]{3,2,1,0:T(8,128)S(1)} %get-tuple-element.241), channel_id=1, source_target_pairs={{0,8},{4,12},{1,9},{5,13},{2,10},{6,14},{3,11},{7,15}} | collective-permute-start | bytes 786440 | tf_op jit(solution)/shard_map/ppermute | solution.py:254
  257.0 13.5 %collective-permute-start.51 = (f32[16,2,16,128]{3,2,1,0:T(8,128)}, f32[16,2,16,128]{3,2,1,0:T(8,128)}, u32[]{:S(2)}, u32[]{:S(2)}) collective-permute-start(f32[16,2,16,128]{3,2,1,0:T(8,128)} %fusion.35), channel_id=1, source_target_pairs={{8,0},{12,4},{16,8},{20,12},{24,16},{28,20},{9,1},{13,5},{17,9},{2... | collective-permute-start | bytes 786440 | tf_op jit(solution)/shard_map/ppermute | solution.py:254
  258.3 13.7 %collective-permute-start.52 = (f32[16,2,16,128]{3,2,1,0:T(8,128)}, f32[16,2,16,128]{3,2,1,0:T(8,128)}, u32[]{:S(2)}, u32[]{:S(2)}) collective-permute-start(f32[16,2,16,128]{3,2,1,0:T(8,128)} %fusion.35), channel_id=1, source_target_pairs={{0,8},{4,12},{8,16},{12,20},{16,24},{20,28},{1,9},{5,13},{9,17},{1... | collective-permute-start | bytes 786440 | tf_op jit(solution)/shard_map/ppermute | solution.py:254
  272.0 13.1 %collective-permute-start.53 = (f32[16,2,16,128]{3,2,1,0:T(8,128)}, f32[16,2,16,128]{3,2,1,0:T(8,128)S(1)}, u32[]{:S(2)}, u32[]{:S(2)}) collective-permute-start(f32[16,2,16,128]{3,2,1,0:T(8,128)} %collective-permute-done.52), channel_id=1, source_target_pairs={{8,16},{12,20},{16,24},{20,28},{9,17},{13,21},{17,25},{21,29},{10,... | collective-permute-start | bytes 786440 | tf_op jit(solution)/shard_map/ppermute | solution.py:254
  275.4 11.1 %collective-permute-start.61 = (f32[16,2,16,128]{3,2,1,0:T(8,128)S(1)}, f32[16,2,16,128]{3,2,1,0:T(8,128)S(1)}, u32[]{:S(2)}, u32[]{:S(2)}) collective-permute-start(f32[16,2,16,128]{3,2,1,0:T(8,128)S(1)} %get-tuple-element.240), channel_id=1, source_target_pairs={{16,8},{20,12},{24,16},{28,20},{17,9},{21,13},{25,17},{29,21},{18,... | collective-permute-start | bytes 786440 | tf_op jit(solution)/shard_map/ppermute | solution.py:254
  278.6 30.2 %collective-permute-start.47 = (f32[8,2,64,128]{3,2,1,0:T(8,128)S(1)}, f32[8,2,64,128]{3,2,1,0:T(8,128)S(1)}, u32[]{:S(2)}, u32[]{:S(2)}) collective-permute-start(f32[8,2,64,128]{3,2,1,0:T(8,128)S(1)} %get-tuple-element.177), channel_id=1, source_target_pairs={{0,1},{1,2},{2,3},{3,0},{4,5},{5,6},{6,7},{7,4},{8,9},{9,10},{10,1... | collective-permute-start | bytes 1572872 | tf_op jit(solution)/shard_map/ppermute | solution.py:240
  278.7 35.1 %collective-permute-start.50 = (f32[4,16,2,16,128]{4,3,2,1,0:T(8,128)S(1)}, f32[4,16,2,16,128]{4,3,2,1,0:T(8,128)S(1)}, u32[]{:S(2)}, u32[]{:S(2)}) collective-permute-start(f32[4,16,2,16,128]{4,3,2,1,0:T(8,128)S(1)} %pad_maximum_fusion.1.refs_0_), channel_id=1, source_target_pairs={{0,4},{4,0},{8,12},{12,8},{16,20},{20,16},{24,28},{28,24},{1,5},{5... | collective-permute-start | bytes 3145736 | tf_op jit(solution)/shard_map/ppermute | solution.py:248
  280.3 18.5 %collective-permute-start.59 = (f32[16,2,16,128]{3,2,1,0:T(8,128)S(1)}, f32[16,2,16,128]{3,2,1,0:T(8,128)S(1)}, u32[]{:S(2)}, u32[]{:S(2)}) collective-permute-start(f32[16,2,16,128]{3,2,1,0:T(8,128)S(1)} %get-tuple-element.239), channel_id=1, source_target_pairs={{0,8},{4,12},{8,16},{12,20},{16,24},{20,28},{1,9},{5,13},{9,17},{1... | collective-permute-start | bytes 786440 | tf_op jit(solution)/shard_map/ppermute | solution.py:254
  285.1 11.1 %collective-permute-start.56 = (f32[16,2,16,128]{3,2,1,0:T(8,128)S(1)}, f32[16,2,16,128]{3,2,1,0:T(8,128)S(1)}, u32[]{:S(2)}, u32[]{:S(2)}) collective-permute-start(f32[16,2,16,128]{3,2,1,0:T(8,128)S(1)} %collective-permute-done.55), channel_id=1, source_target_pairs={{8,0},{12,4},{9,1},{13,5},{10,2},{14,6},{11,3},{15,7}} | collective-permute-start | bytes 786440 | tf_op jit(solution)/shard_map/ppermute | solution.py:254
  286.5 11.5 %collective-permute-start.54 = (f32[16,2,16,128]{3,2,1,0:T(8,128)S(1)}, f32[16,2,16,128]{3,2,1,0:T(8,128)S(1)}, u32[]{:S(2)}, u32[]{:S(2)}) collective-permute-start(f32[16,2,16,128]{3,2,1,0:T(8,128)S(1)} %collective-permute-done.53), channel_id=1, source_target_pairs={{16,24},{20,28},{17,25},{21,29},{18,26},{22,30},{19,27},{23,31}} | collective-permute-start | bytes 786440 | tf_op jit(solution)/shard_map/ppermute | solution.py:254
  296.2 14.0 %collective-permute-start.48 = (f32[8,2,64,128]{3,2,1,0:T(8,128)S(1)}, f32[8,2,64,128]{3,2,1,0:T(8,128)S(1)}, u32[]{:S(2)}, u32[]{:S(2)}) collective-permute-start(f32[8,2,64,128]{3,2,1,0:T(8,128)S(1)} %get-tuple-element.178), channel_id=1, source_target_pairs={{0,2},{1,3},{2,0},{3,1},{4,6},{5,7},{6,4},{7,5},{8,10},{9,11},{10,... | collective-permute-start | bytes 1572872 | tf_op jit(solution)/shard_map/ppermute | solution.py:240
  298.0 15.7 %collective-permute-start.49 = (f32[8,2,64,128]{3,2,1,0:T(8,128)S(1)}, f32[8,2,64,128]{3,2,1,0:T(8,128)S(1)}, u32[]{:S(2)}, u32[]{:S(2)}) collective-permute-start(f32[8,2,64,128]{3,2,1,0:T(8,128)S(1)} %get-tuple-element.179), channel_id=1, source_target_pairs={{0,3},{1,0},{2,1},{3,2},{4,7},{5,4},{6,5},{7,6},{8,11},{9,8},{10,9... | collective-permute-start | bytes 1572872 | tf_op jit(solution)/shard_map/ppermute | solution.py:240
  315.6 10.7 %collective-permute-start.68 = (f32[16,2,16,128]{3,2,1,0:T(8,128)S(1)}, f32[16,2,16,128]{3,2,1,0:T(8,128)S(1)}, u32[]{:S(2)}, u32[]{:S(2)}) collective-permute-start(f32[16,2,16,128]{3,2,1,0:T(8,128)S(1)} %fusion.37), channel_id=1, source_target_pairs={{0,8},{4,12},{8,16},{12,20},{16,24},{20,28},{1,9},{5,13},{9,17},{1... | collective-permute-start | bytes 786440 | tf_op jit(solution)/shard_map/ppermute | solution.py:254
  324.5 10.8 %collective-permute-start.71 = (f32[16,2,16,128]{3,2,1,0:T(8,128)S(1)}, f32[16,2,16,128]{3,2,1,0:T(8,128)S(1)}, u32[]{:S(2)}, u32[]{:S(2)}) collective-permute-start(f32[16,2,16,128]{3,2,1,0:T(8,128)S(1)} %collective-permute-done.67), channel_id=1, source_target_pairs={{8,0},{12,4},{16,8},{20,12},{9,1},{13,5},{17,9},{21,13},{10,2},{14... | collective-permute-start | bytes 786440 | tf_op jit(solution)/shard_map/ppermute | solution.py:254
  326.3 14.3 %collective-permute-start.69 = (f32[16,2,16,128]{3,2,1,0:T(8,128)S(1)}, f32[16,2,16,128]{3,2,1,0:T(8,128)S(1)}, u32[]{:S(2)}, u32[]{:S(2)}) collective-permute-start(f32[16,2,16,128]{3,2,1,0:T(8,128)S(1)} %collective-permute-done.68), channel_id=1, source_target_pairs={{8,16},{12,20},{16,24},{20,28},{9,17},{13,21},{17,25},{21,29},{10,... | collective-permute-start | bytes 786440 | tf_op jit(solution)/shard_map/ppermute | solution.py:254
  327.0 37.4 %collective-permute-start.66 = (f32[4,16,2,16,128]{4,3,2,1,0:T(8,128)S(1)}, f32[4,16,2,16,128]{4,3,2,1,0:T(8,128)S(1)}, u32[]{:S(2)}, u32[]{:S(2)}) collective-permute-start(f32[4,16,2,16,128]{4,3,2,1,0:T(8,128)S(1)} %pad_maximum_fusion.2.refs_0_), channel_id=1, source_target_pairs={{0,4},{4,0},{8,12},{12,8},{16,20},{20,16},{24,28},{28,24},{1,5},{5... | collective-permute-start | bytes 3145736 | tf_op jit(solution)/shard_map/ppermute | solution.py:248
  339.1 13.7 %collective-permute-start.63 = (f32[8,2,64,128]{3,2,1,0:T(8,128)S(1)}, f32[8,2,64,128]{3,2,1,0:T(8,128)S(1)}, u32[]{:S(2)}, u32[]{:S(2)}) collective-permute-start(f32[8,2,64,128]{3,2,1,0:T(8,128)S(1)} %get-tuple-element.187), channel_id=1, source_target_pairs={{0,1},{1,2},{2,3},{3,0},{4,5},{5,6},{6,7},{7,4},{8,9},{9,10},{10,1... | collective-permute-start | bytes 1572872 | tf_op jit(solution)/shard_map/ppermute | solution.py:240
  339.2 14.8 %collective-permute-start.64 = (f32[8,2,64,128]{3,2,1,0:T(8,128)S(1)}, f32[8,2,64,128]{3,2,1,0:T(8,128)S(1)}, u32[]{:S(2)}, u32[]{:S(2)}) collective-permute-start(f32[8,2,64,128]{3,2,1,0:T(8,128)S(1)} %get-tuple-element.188), channel_id=1, source_target_pairs={{0,2},{1,3},{2,0},{3,1},{4,6},{5,7},{6,4},{7,5},{8,10},{9,11},{10,... | collective-permute-start | bytes 1572872 | tf_op jit(solution)/shard_map/ppermute | solution.py:240
  345.2 18.3 %collective-permute-start.65 = (f32[8,2,64,128]{3,2,1,0:T(8,128)S(1)}, f32[8,2,64,128]{3,2,1,0:T(8,128)S(1)}, u32[]{:S(2)}, u32[]{:S(2)}) collective-permute-start(f32[8,2,64,128]{3,2,1,0:T(8,128)S(1)} %get-tuple-element.189), channel_id=1, source_target_pairs={{0,3},{1,0},{2,1},{3,2},{4,7},{5,4},{6,5},{7,6},{8,11},{9,8},{10,9... | collective-permute-start | bytes 1572872 | tf_op jit(solution)/shard_map/ppermute | solution.py:240
  364.3 30.9 %collective-permute-start.76 = (f32[4,16,2,16,128]{4,3,2,1,0:T(8,128)S(1)}, f32[4,16,2,16,128]{4,3,2,1,0:T(8,128)}, u32[]{:S(2)}, u32[]{:S(2)}) collective-permute-start(f32[4,16,2,16,128]{4,3,2,1,0:T(8,128)S(1)} %pad_maximum_fusion.3.refs_0_), channel_id=1, source_target_pairs={{0,4},{4,0},{8,12},{12,8},{16,20},{20,16},{24,28},{28,24},{1,5},{5... | collective-permute-start | bytes 3145736 | tf_op jit(solution)/shard_map/ppermute | solution.py:248
  370.8 12.3 %collective-permute-start.73 = (f32[8,2,64,128]{3,2,1,0:T(8,128)S(1)}, f32[8,2,64,128]{3,2,1,0:T(8,128)S(1)}, u32[]{:S(2)}, u32[]{:S(2)}) collective-permute-start(f32[8,2,64,128]{3,2,1,0:T(8,128)S(1)} %get-tuple-element.195), channel_id=1, source_target_pairs={{0,1},{1,2},{2,3},{3,0},{4,5},{5,6},{6,7},{7,4},{8,9},{9,10},{10,1... | collective-permute-start | bytes 1572872 | tf_op jit(solution)/shard_map/ppermute | solution.py:240
  372.3 14.9 %collective-permute-start.74 = (f32[8,2,64,128]{3,2,1,0:T(8,128)S(1)}, f32[8,2,64,128]{3,2,1,0:T(8,128)S(1)}, u32[]{:S(2)}, u32[]{:S(2)}) collective-permute-start(f32[8,2,64,128]{3,2,1,0:T(8,128)S(1)} %get-tuple-element.196), channel_id=1, source_target_pairs={{0,2},{1,3},{2,0},{3,1},{4,6},{5,7},{6,4},{7,5},{8,10},{9,11},{10,... | collective-permute-start | bytes 1572872 | tf_op jit(solution)/shard_map/ppermute | solution.py:240
  373.1 22.1 %collective-permute-start.75 = (f32[8,2,64,128]{3,2,1,0:T(8,128)S(1)}, f32[8,2,64,128]{3,2,1,0:T(8,128)S(1)}, u32[]{:S(2)}, u32[]{:S(2)}) collective-permute-start(f32[8,2,64,128]{3,2,1,0:T(8,128)S(1)} %get-tuple-element.197), channel_id=1, source_target_pairs={{0,3},{1,0},{2,1},{3,2},{4,7},{5,4},{6,5},{7,6},{8,11},{9,8},{10,9... | collective-permute-start | bytes 1572872 | tf_op jit(solution)/shard_map/ppermute | solution.py:240
  398.7 24.6 %collective-permute-start.77 = (f32[8,2,64,128]{3,2,1,0:T(8,128)S(1)}, f32[8,2,64,128]{3,2,1,0:T(8,128)S(1)}, u32[]{:S(2)}, u32[]{:S(2)}) collective-permute-start(f32[8,2,64,128]{3,2,1,0:T(8,128)S(1)} %get-tuple-element.203), channel_id=1, source_target_pairs={{0,1},{1,2},{2,3},{3,0},{4,5},{5,6},{6,7},{7,4},{8,9},{9,10},{10,1... | collective-permute-start | bytes 1572872 | tf_op jit(solution)/shard_map/ppermute | solution.py:240
  399.7 23.6 %collective-permute-start.78 = (f32[8,2,64,128]{3,2,1,0:T(8,128)S(1)}, f32[8,2,64,128]{3,2,1,0:T(8,128)S(1)}, u32[]{:S(2)}, u32[]{:S(2)}) collective-permute-start(f32[8,2,64,128]{3,2,1,0:T(8,128)S(1)} %get-tuple-element.204), channel_id=1, source_target_pairs={{0,2},{1,3},{2,0},{3,1},{4,6},{5,7},{6,4},{7,5},{8,10},{9,11},{10,... | collective-permute-start | bytes 1572872 | tf_op jit(solution)/shard_map/ppermute | solution.py:240
  401.1 22.2 %collective-permute-start.79 = (f32[8,2,64,128]{3,2,1,0:T(8,128)S(1)}, f32[8,2,64,128]{3,2,1,0:T(8,128)S(1)}, u32[]{:S(2)}, u32[]{:S(2)}) collective-permute-start(f32[8,2,64,128]{3,2,1,0:T(8,128)S(1)} %get-tuple-element.205), channel_id=1, source_target_pairs={{0,3},{1,0},{2,1},{3,2},{4,7},{5,4},{6,5},{7,6},{8,11},{9,8},{10,9... | collective-permute-start | bytes 1572872 | tf_op jit(solution)/shard_map/ppermute | solution.py:240
  (81 other events, 714.7 us)
